TPU v7x, 32 devices: a whole 2x2x4 slice. The times are simulated.
32 devices in a mesh: line: 4 (over x, core), shot: 8 (over z, y).
Axes of the slice: x: 2, y: 2, z: 4, core: 2. Of those that a mesh axis runs over, the one named last changes fastest.
Arguments:
- velocity: float32 [64, 128, 128], P('line', 'shot'), may hold values from 1.5 to 4.5
- density: float32 [64, 128, 128], P('line', 'shot'), may hold values from 1 to 3
- start_pressure: float32 [128, 256, 128], P('line', 'shot'), may hold values from -6 to 6
- observed: float32 [128, 256, 128], P('line', 'shot'), may hold values from -6 to 6
- corners: int32 [4, 8, 2], P('line', 'shot'), may hold values from 0 to 96, as said below
Outputs:
- grad_velocity: float32 [64, 128, 128], P('line', 'shot')
- grad_density: float32 [64, 128, 128], P('line', 'shot')
Inputs may be any that keep to these rules, and one draw needn't show every extreme that they name: corners[a, b, 0] = min(max(a * 16 - 16 + r, 0), 32) and corners[a, b, 1] = min(max(b * 16 - 16 + t, 0), 96) for whole numbers r and t of 0 to 16.
All inputs are finite; a program needn't handle non-finite values.
Results may differ from a plain program's by a relative error of at most 0.0003.
Values sent between devices are 32-bit elements; how exact they have to be, the bound alone decides.
A program may use at most 64 MiB of HBM per device.

v0:
```python
import jax
import jax.numpy as jnp
from jax import lax
from jax.sharding import PartitionSpec as P

coeffs = (1225.0 / 1024.0, -245.0 / 3072.0, 49.0 / 5120.0, -5.0 / 7168.0)
time_ratio = 0.1
wavelet = (20.0, -12.0)


def passed_along(block, axis, distance):
    devices = range(lax.axis_size(axis))
    route = [(i - distance, i) for i in devices if i - distance in devices]
    return lax.ppermute(block, axis, route)


def extended_2(cells, sides, width):
    for axis, dim in sides:
        count = lax.axis_size(axis)
        ends = count - 1
        head = lax.slice_in_dim(cells, 0, width, axis=dim)
        tail = lax.slice_in_dim(cells, cells.shape[dim] - width, cells.shape[dim], axis=dim)
        cells = jnp.concatenate(
            [
                lax.ppermute(tail, axis, [(i, (i + 1) % count) for i in range(ends)]),
                cells,
                lax.ppermute(head, axis, [((i + 1) % count, i) for i in range(ends)]),
            ],
            axis=dim,
        )
    return cells


def deriv_plus(field, axis):
    widths = [(0, 0)] * 3
    widths[axis] = (4, 4)
    padded = jnp.pad(field, widths)
    count = field.shape[axis]
    total = jnp.zeros_like(field)
    for m in range(1, 5):
        upper = lax.slice_in_dim(padded, 4 + m, 4 + m + count, axis=axis)
        lower = lax.slice_in_dim(padded, 5 - m, 5 - m + count, axis=axis)
        total = total + coeffs[m - 1] * (upper - lower)
    return total


def deriv_minus(field, axis):
    widths = [(0, 0)] * 3
    widths[axis] = (4, 4)
    padded = jnp.pad(field, widths)
    count = field.shape[axis]
    total = jnp.zeros_like(field)
    for m in range(1, 5):
        upper = lax.slice_in_dim(padded, 3 + m, 3 + m + count, axis=axis)
        lower = lax.slice_in_dim(padded, 4 - m, 4 - m + count, axis=axis)
        total = total + coeffs[m - 1] * (upper - lower)
    return total


def shot_misfit(model, pressure, observed):
    speed = model[0]
    dense = model[1]
    vel_x = jnp.zeros_like(pressure)
    vel_y = jnp.zeros_like(pressure)
    vel_z = jnp.zeros_like(pressure)
    centre = (pressure.shape[0] // 2, pressure.shape[1] // 2, pressure.shape[2] // 2)
    for level in range(2):
        vel_x = vel_x - time_ratio * deriv_plus(pressure, 0) / dense
        vel_y = vel_y - time_ratio * deriv_plus(pressure, 1) / dense
        vel_z = vel_z - time_ratio * deriv_plus(pressure, 2) / dense
        spread = deriv_minus(vel_x, 0) + deriv_minus(vel_y, 1) + deriv_minus(vel_z, 2)
        pressure = pressure - time_ratio * dense * speed * speed * spread
        pressure = pressure.at[centre].add(wavelet[level])
    misfit_term = pressure - observed
    return 0.5 * jnp.sum(misfit_term * misfit_term)


def return_line(terms, block):
    below = lax.slice_in_dim(terms, 0, block, axis=1)
    middle = lax.slice_in_dim(terms, block, 2 * block, axis=1)
    above = lax.slice_in_dim(terms, 2 * block, 3 * block, axis=1)
    from_prev = passed_along(above, "line", 1)
    from_next = passed_along(below, "line", -1)
    return middle + from_prev + from_next


def return_shot(terms, block):
    below = lax.slice_in_dim(terms, 0, block, axis=2)
    middle = lax.slice_in_dim(terms, block, 2 * block, axis=2)
    above = lax.slice_in_dim(terms, 2 * block, 3 * block, axis=2)
    from_prev = passed_along(above, "shot", 1)
    from_next = passed_along(below, "shot", -1)
    return middle + from_prev + from_next


def body(velocity, density, start_pressure, observed, corners):
    block = velocity.shape[0]
    depth = velocity.shape[2]
    width = start_pressure.shape[0]
    model = jnp.stack([velocity, density])
    extended = extended_2(model, (("line", 1), ("shot", 2)), block)
    line_index = lax.axis_index("line")
    shot_index = lax.axis_index("shot")
    corner = corners[0, 0]
    offset_x = corner[0] - (line_index - 1) * block
    offset_y = corner[1] - (shot_index - 1) * block
    zero_int = jnp.zeros((), jnp.int32)
    place = (zero_int, offset_x, offset_y, zero_int)
    aperture = lax.dynamic_slice(extended, place, (2, width, width, depth))
    local = jax.grad(shot_misfit)(aperture, start_pressure, observed)
    terms = lax.dynamic_update_slice(
        jnp.zeros((2, 3 * block, 3 * block, depth), jnp.float32), local, place
    )
    owned = return_shot(return_line(terms, block), block)
    return (owned[0], owned[1])


def solution(mesh):
    placed = (
        P("line", "shot", None),
        P("line", "shot", None),
        P("line", "shot", None),
        P("line", "shot", None),
        P("line", "shot", None),
    )
    return jax.shard_map(
        body,
        mesh=mesh,
        in_specs=placed,
        out_specs=(P("line", "shot", None), P("line", "shot", None)),
        check_vma=False,
    )
```

profile of v0, /device:TPU:9, one launch (start us, length us, event | category | flops | bytes accessed | tf_op | source)
XLA Modules:
  0.0 105.9 jit_solution(1865744108315864150)
XLA Ops:
  0.6 1.0 pad_maximum_fusion.1
  1.6 3.8 %collective-permute-start = (f32[2,16,16,128]{3,2,1,0:T(8,128)S(1)}, f32[2,16,16,128]{3,2,1,0:T(8,128)S(1)}, u32[]{:S(2)}, u32[]{:S(2)}) collective-permute-start(f32[2,16,16,128]{3,2,1,0:T(8,128)S(1)} %pad_maximum_fusion.1), channel_id=1, source_target_pairs={{0,8},{8,16},{16,24},{1,9},{9,17},{17,25},{2,10},{10,18},{18,26},{... | collective-permute-start | bytes 786440 | tf_op jit(solution)/shard_map/ppermute | solution.py:25
  5.5 1.9 %collective-permute-start.1 = (f32[2,16,16,128]{3,2,1,0:T(8,128)S(1)}, f32[2,16,16,128]{3,2,1,0:T(8,128)S(1)}, u32[]{:S(2)}, u32[]{:S(2)}) collective-permute-start(f32[2,16,16,128]{3,2,1,0:T(8,128)S(1)} %pad_maximum_fusion.1), channel_id=1, source_target_pairs={{8,0},{16,8},{24,16},{9,1},{17,9},{25,17},{10,2},{18,10},{26,18},{... | collective-permute-start | bytes 786440 | tf_op jit(solution)/shard_map/ppermute | solution.py:27
  7.4 1.4 %collective-permute-done = f32[2,16,16,128]{3,2,1,0:T(8,128)S(1)} collective-permute-done((f32[2,16,16,128]{3,2,1,0:T(8,128)S(1)}, f32[2,16,16,128]{3,2,1,0:T(8,128)S(1)}, u32[]{:S(2)}, u32[]{:S(2)}) %collective-permute-start) | collective-permute-done | bytes 262176 | tf_op jit(solution)/shard_map/ppermute | solution.py:25
  8.7 4.4 %collective-permute-done.1 = f32[2,16,16,128]{3,2,1,0:T(8,128)S(1)} collective-permute-done((f32[2,16,16,128]{3,2,1,0:T(8,128)S(1)}, f32[2,16,16,128]{3,2,1,0:T(8,128)S(1)}, u32[]{:S(2)}, u32[]{:S(2)}) %collective-permute-start.1) | collective-permute-done | bytes 262176 | tf_op jit(solution)/shard_map/ppermute | solution.py:27
  13.1 1.0 pad_maximum_fusion
  14.2 3.1 %collective-permute-start.2 = (f32[2,48,16,128]{3,2,1,0:T(8,128)S(1)}, f32[2,48,16,128]{3,2,1,0:T(8,128)S(1)}, u32[]{:S(2)}, u32[]{:S(2)}) collective-permute-start(f32[2,48,16,128]{3,2,1,0:T(8,128)S(1)} %pad_maximum_fusion), channel_id=1, source_target_pairs={{0,1},{1,2},{2,3},{3,4},{4,5},{5,6},{6,7},{8,9},{9,10},{10,11},{11... | collective-permute-start | bytes 2359304 | tf_op jit(solution)/shard_map/ppermute | solution.py:25
  17.3 3.0 %collective-permute-start.3 = (f32[2,48,16,128]{3,2,1,0:T(8,128)S(1)}, f32[2,48,16,128]{3,2,1,0:T(8,128)}, u32[]{:S(2)}, u32[]{:S(2)}) collective-permute-start(f32[2,48,16,128]{3,2,1,0:T(8,128)S(1)} %pad_maximum_fusion), channel_id=1, source_target_pairs={{1,0},{2,1},{3,2},{4,3},{5,4},{6,5},{7,6},{9,8},{10,9},{11,10},{12... | collective-permute-start | bytes 2359304 | tf_op jit(solution)/shard_map/ppermute | solution.py:27
  20.4 1.3 %fusion.271 = (s32[1,1,1]{2,1,0:T(1,128)}, s32[1,1,1]{2,1,0:T(1,128)}) fusion(s32[1,1,2]{2,1,0:T(1,128)} %param.13), kind=kLoop, calls=%fused_computation.411 | loop fusion | bytes 16 | tf_op jit(solution)/shard_map/slice | solution.py:106
  23.0 24.7 %collective-permute-done.2 = f32[2,48,16,128]{3,2,1,0:T(8,128)S(1)} collective-permute-done((f32[2,48,16,128]{3,2,1,0:T(8,128)S(1)}, f32[2,48,16,128]{3,2,1,0:T(8,128)S(1)}, u32[]{:S(2)}, u32[]{:S(2)}) %collective-permute-start.2) | collective-permute-done | bytes 786464 | tf_op jit(solution)/shard_map/ppermute | solution.py:25
  47.7 1.9 %collective-permute-done.3 = f32[2,48,16,128]{3,2,1,0:T(8,128)} collective-permute-done((f32[2,48,16,128]{3,2,1,0:T(8,128)S(1)}, f32[2,48,16,128]{3,2,1,0:T(8,128)}, u32[]{:S(2)}, u32[]{:S(2)}) %collective-permute-start.3) | collective-permute-done | bytes 786464 | tf_op jit(solution)/shard_map/ppermute | solution.py:27
  49.6 1.9 %fusion.1 = f32[2,32,32,128]{3,2,1,0:T(8,128)S(1)} fusion(s32[]{:T(128)S(6)} %select_n.8, s32[]{:T(128)S(6)} %select_n.9, f32[2,48,16,128]{3,2,1,0:T(8,128)S(1)} %collective-permute-done.2, f32[2,16,16,128]{3,2,1,0:T(8,128)S(1)} %collective-permute-done, f32[1,16,16,128]{3,2,1,0:T(8,128)} %bitcast.56, f32[1,16,16,128]{3,2,1,0:T(8,128)} %bitcast.53, ...), kind=kLoop, calls=%fused_computation.35 | loop fusion | flops 1310720 | bytes 3407880 | tf_op jit(solution)/shard_map/concatenate | solution.py:23
  51.5 2.3 %divide_subtract_fusion.5 = (f32[32,32,128]{2,1,0:T(8,128)S(1)}, f32[32,32,128]{2,1,0:T(8,128)}, f32[32,32,128]{2,1,0:T(8,128)S(1)}, f32[32,32,128]{2,1,0:T(8,12...) fusion(f32[2,32,32,128]{3,2,1,0:T(8,128)S(1)} %fusion.1, f32[32,32,128]{2,1,0:T(8,128)S(1)} %copy-done.3), kind=kLoop, calls=%fused_computation.356 | loop fusion | flops 5505024 | bytes 4194304 | tf_op jit(solution)/shard_map/jvp()/sub | solution.py:68
  53.8 1.1 multiply_subtract_fusion.1
  54.8 0.6 slice.462
  56.1 0.1 scatter-add.6
  56.2 3.4 %divide_subtract_fusion.2 = (f32[32,32,128]{2,1,0:T(8,128)S(1)}, f32[32,32,128]{2,1,0:T(8,128)}, f32[32,32,128]{2,1,0:T(8,128)S(1)}, f32[32,32,128]{2,1,0:T(8,12...) fusion(f32[32,32,128]{2,1,0:T(8,128)S(1)} %get-tuple-element.56, f32[2,32,32,128]{3,2,1,0:T(8,128)S(1)} %fusion.1, ...), kind=kLoop, calls=%fused_computation.352 | loop fusion | flops 5505024 | bytes 5767168 | tf_op jit(solution)/shard_map/jvp()/sub | solution.py:68
  59.7 1.1 multiply_subtract_fusion
  60.7 0.8 copy-done.2
  61.5 0.6 slice.463
  62.7 1.5 %scatter-add.9 = f32[32,32,128]{2,1,0:T(8,128)} dynamic-update-slice(f32[32,32,128]{2,1,0:T(8,128)} %copy-done.2, f32[1,1,1]{2,1,0:T(1,128)S(6)} %add.372, s32[]{:T(128)} %constant.103.clone.1, s32[]{:T(128)} %constant.103.clone.1, s32[]{:T(128)} %constant.112.clone.1) | dynamic-update-slice | bytes 12 | tf_op jit(solution)/shard_map/jvp()/scatter-add | solution.py:73
  64.2 1.4 %broadcast_multiply_fusion.18 = (f32[32,32,128]{2,1,0:T(8,128)S(1)}, f32[32,32,128]{2,1,0:T(8,128)S(1)}, f32[32,32,128]{2,1,0:T(8,128)S(1)}) fusion(f32[32,32,128]{2,1,0:T(8,128)S(1)} %get-tuple-element.51, f32[32,32,128]{2,1,0:T(8,128)} %scatter-add.9, f32[32,32,128]{2,1,0:T(8,128)} %param.12), kind=kLoop, calls=%fused_computation.385 | loop fusion | flops 786432 | bytes 3145728 | tf_op jit(solution)/shard_map/transpose(jvp())/mul | solution.py:56
  65.6 0.5 fusion.243
  66.1 1.2 %fusion.247 = (f32[32,32,128]{2,1,0:T(8,128)S(1)}, f32[32,32,128]{2,1,0:T(8,128)S(1)}, f32[32,32,128]{2,1,0:T(8,128)S(1)}, f32[32,32,128]{2,1,0:T(8,128)S(1)}, f...) fusion(f32[2,32,32,128]{3,2,1,0:T(8,128)S(1)} %fusion.1, f32[32,32,128]{2,1,0:T(8,128)S(1)} %get-tuple-element.38, ...), kind=kLoop, calls=%fused_computation.400 | loop fusion | flops 2883584 | bytes 7864320 | tf_op jit(solution)/shard_map/transpose(jvp())/neg | solution.py:43
  67.3 0.5 fusion.249
  67.8 0.5 fusion.246
  68.3 0.9 fusion.244
  69.2 1.6 %broadcast_multiply_fusion.19 = (f32[32,32,128]{2,1,0:T(8,128)S(1)}, f32[32,32,128]{2,1,0:T(8,128)S(1)}, f32[32,32,128]{2,1,0:T(8,128)S(1)}) fusion(f32[32,32,128]{2,1,0:T(8,128)S(1)} %get-tuple-element.51, f32[32,32,128]{2,1,0:T(8,128)S(1)} %get-tuple-element.97, f32[32,32,128]{2,1,0:T(8,128)S(1)} %get-tuple-element.96, ...), kind=kLoop, calls=%fused_computation.386 | loop fusion | flops 3538944 | bytes 15204352 | tf_op jit(solution)/shard_map/transpose(jvp())/mul | solution.py:56
  70.9 0.5 fusion.237
  71.4 0.4 add_bitcast_fusion
  71.8 0.6 copy-done.5
  72.4 0.2 copy-done.6
  72.6 0.2 copy-done.7
  72.7 0.2 copy-done.8
  72.9 0.2 copy-done.9
  73.0 0.2 copy-done.10
  73.2 2.5 %fusion.51 = f32[1,32,32,128]{3,2,1,0:T(8,128)S(1)} fusion(f32[32,32,128]{2,1,0:T(8,128)S(1)} %copy-done.6, f32[32,32,128]{2,1,0:T(8,128)S(1)} %get-tuple-element.60, f32[32,32,128]{2,1,0:T(8,128)S(1)} %get-tuple-element.75, f32[32,32,128]{2,1,0:T(8,128)S(1)} %get-tuple-element.79, f32[32,32,128]{2,1,0:T(8,128)S(1)} %copy-done.5, ...), kind=kLoop, calls=%fused_computation.162 | loop fusion | flops 8650752 | bytes 12582912 | tf_op jit(solution)/shard_map/transpose(jvp())/broadcast_in_dim | solution.py:62
  75.8 0.2 broadcast_in_dim.13
  76.0 2.5 %dynamic_update_slice.3 = f32[2,48,48,128]{3,2,1,0:T(8,128)S(1)} dynamic-update-slice(f32[2,48,48,128]{3,2,1,0:T(8,128)S(1)} %broadcast_in_dim.13, f32[2,32,32,128]{3,2,1,0:T(8,128)S(1)} %pad_add_fusion, s32[]{:T(128)} %constant.100.clone.1, s32[]{:T(128)S(6)} %select_n.8, s32[]{:T(128)S(6)} %select_n.9, s32[]{:T(128)} %constant.100.clone.1) | dynamic-update-slice | bytes 2097156 | tf_op jit(solution)/shard_map/dynamic_update_slice | solution.py:111
  78.6 1.9 %collective-permute-start.4 = (f32[2,16,48,128]{3,2,1,0:T(8,128)S(1)}, f32[2,16,48,128]{3,2,1,0:T(8,128)S(1)}, u32[]{:S(2)}, u32[]{:S(2)}) collective-permute-start(f32[2,16,48,128]{3,2,1,0:T(8,128)S(1)} %get-tuple-element.61), channel_id=1, source_target_pairs={{0,8},{8,16},{16,24},{1,9},{9,17},{17,25},{2,10},{10,18},{18,26},{... | collective-permute-start | bytes 2359304 | tf_op jit(solution)/shard_map/ppermute | solution.py:14
  80.5 2.5 %collective-permute-start.5 = (f32[2,16,48,128]{3,2,1,0:T(8,128)S(1)}, f32[2,16,48,128]{3,2,1,0:T(8,128)S(1)}, u32[]{:S(2)}, u32[]{:S(2)}) collective-permute-start(f32[2,16,48,128]{3,2,1,0:T(8,128)S(1)} %get-tuple-element.62), channel_id=1, source_target_pairs={{8,0},{16,8},{24,16},{9,1},{17,9},{25,17},{10,2},{18,10},{26,18},{... | collective-permute-start | bytes 2359304 | tf_op jit(solution)/shard_map/ppermute | solution.py:14
  83.0 6.5 %collective-permute-done.4 = f32[2,16,48,128]{3,2,1,0:T(8,128)S(1)} collective-permute-done((f32[2,16,48,128]{3,2,1,0:T(8,128)S(1)}, f32[2,16,48,128]{3,2,1,0:T(8,128)S(1)}, u32[]{:S(2)}, u32[]{:S(2)}) %collective-permute-start.4) | collective-permute-done | bytes 786464 | tf_op jit(solution)/shard_map/ppermute | solution.py:14
  89.5 4.7 %collective-permute-done.5 = f32[2,16,48,128]{3,2,1,0:T(8,128)S(1)} collective-permute-done((f32[2,16,48,128]{3,2,1,0:T(8,128)S(1)}, f32[2,16,48,128]{3,2,1,0:T(8,128)S(1)}, u32[]{:S(2)}, u32[]{:S(2)}) %collective-permute-start.5) | collective-permute-done | bytes 786464 | tf_op jit(solution)/shard_map/ppermute | solution.py:14
  94.3 1.9 %collective-permute-start.6 = (f32[2,16,16,128]{3,2,1,0:T(8,128)S(1)}, f32[2,16,16,128]{3,2,1,0:T(8,128)S(1)}, u32[]{:S(2)}, u32[]{:S(2)}) collective-permute-start(f32[2,16,16,128]{3,2,1,0:T(8,128)S(1)} %get-tuple-element.71), channel_id=1, source_target_pairs={{0,1},{1,2},{2,3},{3,4},{4,5},{5,6},{6,7},{8,9},{9,10},{10,11},{11... | collective-permute-start | bytes 786440 | tf_op jit(solution)/shard_map/ppermute | solution.py:14
  96.3 4.3 %collective-permute-start.7 = (f32[2,16,16,128]{3,2,1,0:T(8,128)S(1)}, f32[2,16,16,128]{3,2,1,0:T(8,128)S(1)}, u32[]{:S(2)}, u32[]{:S(2)}) collective-permute-start(f32[2,16,16,128]{3,2,1,0:T(8,128)S(1)} %get-tuple-element.72), channel_id=1, source_target_pairs={{1,0},{2,1},{3,2},{4,3},{5,4},{6,5},{7,6},{9,8},{10,9},{11,10},{12... | collective-permute-start | bytes 786440 | tf_op jit(solution)/shard_map/ppermute | solution.py:14
  100.5 1.9 %collective-permute-done.6 = f32[2,16,16,128]{3,2,1,0:T(8,128)S(1)} collective-permute-done((f32[2,16,16,128]{3,2,1,0:T(8,128)S(1)}, f32[2,16,16,128]{3,2,1,0:T(8,128)S(1)}, u32[]{:S(2)}, u32[]{:S(2)}) %collective-permute-start.6) | collective-permute-done | bytes 262176 | tf_op jit(solution)/shard_map/ppermute | solution.py:14
  102.4 2.7 %collective-permute-done.7 = f32[2,16,16,128]{3,2,1,0:T(8,128)S(1)} collective-permute-done((f32[2,16,16,128]{3,2,1,0:T(8,128)S(1)}, f32[2,16,16,128]{3,2,1,0:T(8,128)S(1)}, u32[]{:S(2)}, u32[]{:S(2)}) %collective-permute-start.7) | collective-permute-done | bytes 262176 | tf_op jit(solution)/shard_map/ppermute | solution.py:14
  105.2 0.7 slice_bitcast_fusion.2
  (20 shorter events, 0.5 us)
Async XLA Ops:
  1.6 49.8 %copy-start.3 = (f32[32,32,128]{2,1,0:T(8,128)S(1)}, f32[32,32,128]{2,1,0:T(8,128)}, u32[]{:S(2)}) copy-start(f32[32,32,128]{2,1,0:T(8,128)} %param.11) | copy-start | bytes 1572868
  1.6 7.1 %collective-permute-start = (f32[2,16,16,128]{3,2,1,0:T(8,128)S(1)}, f32[2,16,16,128]{3,2,1,0:T(8,128)S(1)}, u32[]{:S(2)}, u32[]{:S(2)}) collective-permute-start(f32[2,16,16,128]{3,2,1,0:T(8,128)S(1)} %pad_maximum_fusion.1), channel_id=1, source_target_pairs={{0,8},{8,16},{16,24},{1,9},{9,17},{17,25},{2,10},{10,18},{18,26},{... | collective-permute-start | bytes 786440 | tf_op jit(solution)/shard_map/ppermute | solution.py:25
  5.5 7.7 %collective-permute-start.1 = (f32[2,16,16,128]{3,2,1,0:T(8,128)S(1)}, f32[2,16,16,128]{3,2,1,0:T(8,128)S(1)}, u32[]{:S(2)}, u32[]{:S(2)}) collective-permute-start(f32[2,16,16,128]{3,2,1,0:T(8,128)S(1)} %pad_maximum_fusion.1), channel_id=1, source_target_pairs={{8,0},{16,8},{24,16},{9,1},{17,9},{25,17},{10,2},{18,10},{26,18},{... | collective-permute-start | bytes 786440 | tf_op jit(solution)/shard_map/ppermute | solution.py:27
  14.2 33.6 %collective-permute-start.2 = (f32[2,48,16,128]{3,2,1,0:T(8,128)S(1)}, f32[2,48,16,128]{3,2,1,0:T(8,128)S(1)}, u32[]{:S(2)}, u32[]{:S(2)}) collective-permute-start(f32[2,48,16,128]{3,2,1,0:T(8,128)S(1)} %pad_maximum_fusion), channel_id=1, source_target_pairs={{0,1},{1,2},{2,3},{3,4},{4,5},{5,6},{6,7},{8,9},{9,10},{10,11},{11... | collective-permute-start | bytes 2359304 | tf_op jit(solution)/shard_map/ppermute | solution.py:25
  17.3 32.3 %collective-permute-start.3 = (f32[2,48,16,128]{3,2,1,0:T(8,128)S(1)}, f32[2,48,16,128]{3,2,1,0:T(8,128)}, u32[]{:S(2)}, u32[]{:S(2)}) collective-permute-start(f32[2,48,16,128]{3,2,1,0:T(8,128)S(1)} %pad_maximum_fusion), channel_id=1, source_target_pairs={{1,0},{2,1},{3,2},{4,3},{5,4},{6,5},{7,6},{9,8},{10,9},{11,10},{12... | collective-permute-start | bytes 2359304 | tf_op jit(solution)/shard_map/ppermute | solution.py:27
  51.5 2.3 %copy-start.4 = (f32[32,32,128]{2,1,0:T(8,128)S(1)}, f32[32,32,128]{2,1,0:T(8,128)}, u32[]{:S(2)}) copy-start(f32[32,32,128]{2,1,0:T(8,128)} %param.11) | copy-start | bytes 1572868
  53.8 1.1 %copy-start = (f32[32,32,128]{2,1,0:T(8,128)}, f32[32,32,128]{2,1,0:T(8,128)S(1)}, u32[]{:S(2)}) copy-start(f32[32,32,128]{2,1,0:T(8,128)S(1)} %get-tuple-element.67) | copy-start | bytes 1572868
  53.8 1.1 %copy-start.1 = (f32[32,32,128]{2,1,0:T(8,128)}, f32[32,32,128]{2,1,0:T(8,128)S(1)}, u32[]{:S(2)}) copy-start(f32[32,32,128]{2,1,0:T(8,128)S(1)} %get-tuple-element.69) | copy-start | bytes 1572868
  60.7 0.8 copy-start.2
  71.4 1.0 copy-start.5
  71.4 1.2 %copy-start.6 = (f32[32,32,128]{2,1,0:T(8,128)S(1)}, f32[32,32,128]{2,1,0:T(8,128)}, u32[]{:S(2)}) copy-start(f32[32,32,128]{2,1,0:T(8,128)} %get-tuple-element.68) | copy-start | bytes 1572868
  71.4 1.3 %copy-start.7 = (f32[32,32,128]{2,1,0:T(8,128)S(1)}, f32[32,32,128]{2,1,0:T(8,128)}, u32[]{:S(2)}) copy-start(f32[32,32,128]{2,1,0:T(8,128)} %get-tuple-element.70) | copy-start | bytes 1572868
  71.4 1.5 %copy-start.8 = (f32[32,32,128]{2,1,0:T(8,128)S(1)}, f32[32,32,128]{2,1,0:T(8,128)}, u32[]{:S(2)}) copy-start(f32[32,32,128]{2,1,0:T(8,128)} %get-tuple-element.48) | copy-start | bytes 1572868
  71.4 1.6 %copy-start.9 = (f32[32,32,128]{2,1,0:T(8,128)S(1)}, f32[32,32,128]{2,1,0:T(8,128)}, u32[]{:S(2)}) copy-start(f32[32,32,128]{2,1,0:T(8,128)} %get-tuple-element.64) | copy-start | bytes 1572868
  71.4 1.8 %copy-start.10 = (f32[32,32,128]{2,1,0:T(8,128)S(1)}, f32[32,32,128]{2,1,0:T(8,128)}, u32[]{:S(2)}) copy-start(f32[32,32,128]{2,1,0:T(8,128)} %get-tuple-element.66) | copy-start | bytes 1572868
  78.6 10.8 %collective-permute-start.4 = (f32[2,16,48,128]{3,2,1,0:T(8,128)S(1)}, f32[2,16,48,128]{3,2,1,0:T(8,128)S(1)}, u32[]{:S(2)}, u32[]{:S(2)}) collective-permute-start(f32[2,16,48,128]{3,2,1,0:T(8,128)S(1)} %get-tuple-element.61), channel_id=1, source_target_pairs={{0,8},{8,16},{16,24},{1,9},{9,17},{17,25},{2,10},{10,18},{18,26},{... | collective-permute-start | bytes 2359304 | tf_op jit(solution)/shard_map/ppermute | solution.py:14
  80.5 13.6 %collective-permute-start.5 = (f32[2,16,48,128]{3,2,1,0:T(8,128)S(1)}, f32[2,16,48,128]{3,2,1,0:T(8,128)S(1)}, u32[]{:S(2)}, u32[]{:S(2)}) collective-permute-start(f32[2,16,48,128]{3,2,1,0:T(8,128)S(1)} %get-tuple-element.62), channel_id=1, source_target_pairs={{8,0},{16,8},{24,16},{9,1},{17,9},{25,17},{10,2},{18,10},{26,18},{... | collective-permute-start | bytes 2359304 | tf_op jit(solution)/shard_map/ppermute | solution.py:14
  94.3 8.1 %collective-permute-start.6 = (f32[2,16,16,128]{3,2,1,0:T(8,128)S(1)}, f32[2,16,16,128]{3,2,1,0:T(8,128)S(1)}, u32[]{:S(2)}, u32[]{:S(2)}) collective-permute-start(f32[2,16,16,128]{3,2,1,0:T(8,128)S(1)} %get-tuple-element.71), channel_id=1, source_target_pairs={{0,1},{1,2},{2,3},{3,4},{4,5},{5,6},{6,7},{8,9},{9,10},{10,11},{11... | collective-permute-start | bytes 786440 | tf_op jit(solution)/shard_map/ppermute | solution.py:14
  96.3 8.9 %collective-permute-start.7 = (f32[2,16,16,128]{3,2,1,0:T(8,128)S(1)}, f32[2,16,16,128]{3,2,1,0:T(8,128)S(1)}, u32[]{:S(2)}, u32[]{:S(2)}) collective-permute-start(f32[2,16,16,128]{3,2,1,0:T(8,128)S(1)} %get-tuple-element.72), channel_id=1, source_target_pairs={{1,0},{2,1},{3,2},{4,3},{5,4},{6,5},{7,6},{9,8},{10,9},{11,10},{12... | collective-permute-start | bytes 786440 | tf_op jit(solution)/shard_map/ppermute | solution.py:14
where the time goes:
time: 107 us; the launch traced here: 106 us
  waiting for transfers between devices  48.1 us (45%)
  starting transfers between devices  22.5 us (21%)
  other arithmetic  21.9 us (20%)
  local copies, waits for them, and re-layouts  9.85 us (9%)
  between operations  3.56 us (3%)
    ppermute x2, waiting for transfers between devices, extended_2(): lax.ppermute(tail, axis, [(i, (i + 1) % count) for i in range(ends)])  26.1 us
    ppermute x4, waiting for transfers between devices, passed_along(): return lax.ppermute(block, axis, route)  15.8 us
    ppermute x4, starting transfers between devices, passed_along(): return lax.ppermute(block, axis, route)  10.6 us
    ppermute x2, starting transfers between devices, extended_2(): lax.ppermute(tail, axis, [(i, (i + 1) % count) for i in range(ends)])  6.96 us
    ppermute x2, waiting for transfers between devices, extended_2(): lax.ppermute(head, axis, [((i + 1) % count, i) for i in range(ends)])  6.26 us
    sub x2, other arithmetic, shot_misfit(): vel_x = vel_x - time_ratio * deriv_plus(pressure, 0) / dense  5.7 us
    ppermute x2, starting transfers between devices, extended_2(): lax.ppermute(head, axis, [((i + 1) % count, i) for i in range(ends)])  4.96 us
    neg x4, other arithmetic, deriv_plus(): total = total + coeffs[m - 1] * (upper - lower)  3.07 us
  transfers between devices with their start and end apart: 8, of which 8 were waited for; matrix products, arithmetic and copies ran while one was open for 1% of the time, Pallas kernels for 0%

commit v1 on v0

v1 whole, which is shorter than its diff:
```python
import functools

import jax
import jax.numpy as jnp
import ml_dtypes
import numpy as np
from jax import lax
from jax.experimental import pallas as pl
from jax.experimental.pallas import tpu as pltpu
from jax.sharding import PartitionSpec as P

MESH = pl.DeviceIdType.MESH
coeffs = (1225.0 / 1024.0, -245.0 / 3072.0, 49.0 / 5120.0, -5.0 / 7168.0)
time_ratio = 0.1
wavelet = (20.0, -12.0)
RB = 4


def split(value):
    high = float(np.float32(value).astype(ml_dtypes.bfloat16))
    low = float(np.float32(value - high).astype(ml_dtypes.bfloat16))
    return high, low


def band(depth, plus):
    row = lax.broadcasted_iota(jnp.int32, (depth, depth), 0)
    col = lax.broadcasted_iota(jnp.int32, (depth, depth), 1)
    gap = row - col
    high = jnp.zeros((depth, depth), jnp.float32)
    low = jnp.zeros((depth, depth), jnp.float32)
    for m in range(1, 5):
        hi, lo = split(coeffs[m - 1])
        up, down = (m, 1 - m) if plus else (m - 1, -m)
        high = jnp.where(gap == up, hi, jnp.where(gap == down, -hi, high))
        low = jnp.where(gap == up, lo, jnp.where(gap == down, -lo, low))
    top = jnp.concatenate([high, low], axis=1)
    bottom = jnp.concatenate([high, jnp.zeros_like(low)], axis=1)
    return jnp.concatenate([top, bottom], axis=0).astype(jnp.bfloat16)


def along_z(rows, matrix):
    depth = rows[0].shape[1]
    width = rows[0].shape[0]
    field = jnp.concatenate(rows, axis=0)
    high = field.astype(jnp.bfloat16)
    low = (field - high.astype(jnp.float32)).astype(jnp.bfloat16)
    both = jnp.concatenate([high, low], axis=1)
    out = jnp.dot(both, matrix, preferred_element_type=jnp.float32)
    out = out[:, :depth] + out[:, depth:]
    return [out[k * width:(k + 1) * width] for k in range(len(rows))]


def combine(pairs):
    total = None
    for c, (upper, lower) in zip(coeffs, pairs):
        term = c * (upper - lower)
        total = term if total is None else total + term
    return total


def kernel(
    n_line, n_shot,
    corner, vel_in, rho_in, p_in, obs_in,
    vel_out, rho_out,
    ext_v, ext_r, grad_v, grad_r,
    p0, p1, a2, a1, vx1, vx2, bx, vy1, vy2, by,
    ex, ey, ez, zd, inv, kk, s1, ss, q2, vz1, vz2, rr, obs, w_plus, w_minus,
    sl, rl, zs, zr, ys, yr,
    fy_s, fy_r, fz_s, fz_r, fl_s, fl_r, rl_s, rl_r, rz_s, rz_r, ry_s, ry_r,
):
    block, _, depth = vel_in.shape
    width = p_in.shape[0]
    a = lax.axis_index("line")
    b = lax.axis_index("shot")
    odd = lax.rem(b, 2)
    partner = b + 1 - 2 * odd
    onward = b + 2 - 4 * odd
    behind = b - 2 + 4 * odd
    has_onward = (onward >= 0) & (onward < n_shot)
    has_behind = (behind >= 0) & (behind < n_shot)
    line_to = (a - 1, a + 1)
    has_line = (a > 0, a < n_line - 1)
    near = 2 * (1 - odd)
    far = 2 * odd
    exts = (ext_v, ext_r)
    ins = (vel_in, rho_in)
    outs = (vel_out, rho_out)
    grads = (grad_v, grad_r)

    barrier = pltpu.get_barrier_semaphore()

    def greet(there):
        pl.semaphore_signal(barrier, inc=1, device_id=there, device_id_type=MESH)

    greet((a, partner))
    pl.when(has_onward)(lambda: greet((a, onward)))
    pl.when(has_behind)(lambda: greet((a, behind)))
    pl.when(has_line[0])(lambda: greet((a - 1, b)))
    pl.when(has_line[1])(lambda: greet((a + 1, b)))
    one = jnp.int32(1)
    none = jnp.int32(0)
    count = one
    for there in (has_onward, has_behind, has_line[0], has_line[1]):
        count = count + jnp.where(there, one, none)
    pl.semaphore_wait(barrier, count)

    def cols(slot):
        return pl.ds(pl.multiple_of(slot * block, block), block)

    mid = pl.ds(block, block)

    def remote(src, dst, send, recv, there):
        return pltpu.make_async_remote_copy(
            src_ref=src, dst_ref=dst, send_sem=send, recv_sem=recv,
            device_id=there, device_id_type=MESH,
        )

    def fwd_y(k):
        return remote(ins[k], exts[k].at[mid, cols(far), :], fy_s.at[k], fy_r.at[k], (a, partner))

    def fwd_z(k):
        return remote(
            exts[k].at[mid, cols(near), :], exts[k].at[mid, cols(far), :],
            fz_s.at[k], fz_r.at[k], (a, onward),
        )

    def fwd_line(k, piece, side):
        slot = (1, near, far)[piece]
        src = ins[k] if piece == 0 else exts[k].at[mid, cols(slot), :]
        dst = exts[k].at[pl.ds(2 * block * (1 - side), block), cols(slot), :]
        return remote(
            src, dst, fl_s.at[k, piece, side], fl_r.at[k, piece, side], (line_to[side], b)
        )

    def start_line(k, piece):
        for side in range(2):
            pl.when(has_line[side])(lambda side=side: fwd_line(k, piece, side).start())

    for k in (1, 0):
        fwd_y(k).start()
        start_line(k, 0)

    for k in range(2):
        exts[k][block:2 * block, block:2 * block, :] = ins[k][...]
    for field in (p0, p1, a2, a1):
        field[0:4, :, :] = jnp.zeros((4, width + 16, depth), jnp.float32)
        field[width + 4:width + 8, :, :] = jnp.zeros((4, width + 16, depth), jnp.float32)
    for field in (vx1, vx2, bx):
        field[0:4, :, :] = jnp.zeros((4, width, depth), jnp.float32)
        field[width + 4:width + 8, :, :] = jnp.zeros((4, width, depth), jnp.float32)

    def clear(i, carry):
        nothing = jnp.zeros((8, depth), jnp.float32)
        for field, at in ((p0, 4), (p1, 4), (a2, 4), (a1, 4), (vy1, 0), (vy2, 0), (by, 0)):
            field[i + at, 0:8, :] = nothing
            field[i + at, width + 8:width + 16, :] = nothing
        p0[i + 4, 8:width + 8, :] = p_in[i]
        obs[i] = obs_in[i]
        return carry

    lax.fori_loop(0, width, clear, 0)
    w_plus[...] = band(depth, True)
    w_minus[...] = band(depth, False)
    wide = 2 * block + width
    for grad in grads:
        def clear_grad(i, carry, grad=grad):
            grad[i] = jnp.zeros((wide, depth), jnp.float32)
            return carry
        lax.fori_loop(0, wide, clear_grad, 0)

    steps = width // RB

    def over(step):
        def body(i, carry):
            step([i * RB + k for k in range(RB)])
            return carry
        lax.fori_loop(0, steps, body, 0)

    def dx_plus(f, i):
        return combine([(f[i + 4 + m, 8:width + 8, :], f[i + 5 - m, 8:width + 8, :]) for m in range(1, 5)])

    def dy_plus(f, i):
        return combine([(f[i + 4, 8 + m:width + 8 + m, :], f[i + 4, 9 - m:width + 9 - m, :]) for m in range(1, 5)])

    def dx_minus(f, i):
        return combine([(f[i + 3 + m], f[i + 4 - m]) for m in range(1, 5)])

    def dy_minus(f, i):
        return combine([(f[i, 7 + m:width + 7 + m, :], f[i, 8 - m:width + 8 - m, :]) for m in range(1, 5)])

    def body_rows(f, i):
        return f[i + 4, 8:width + 8, :]

    def put_rows(f, i, value):
        f[i + 4, 8:width + 8, :] = value

    def stage_a(rows):
        z = along_z([p_in[i] for i in rows], w_plus[...])
        for i, dz in zip(rows, z):
            ex[i] = dx_plus(p0, i)
            ey[i] = dy_plus(p0, i)
            ez[i] = dz

    over(stage_a)
    lane = lax.broadcasted_iota(jnp.int32, (1, depth), 1)
    spot = jnp.where(lane == depth // 2, 1.0, 0.0).astype(jnp.float32)
    half = width // 2
    p0[half + 4, half + 8:half + 9, :] = p0[half + 4, half + 8:half + 9, :] + wavelet[0] * spot
    obs[half, half:half + 1, :] = obs[half, half:half + 1, :] - wavelet[1] * spot

    for k in (1, 0):
        fwd_y(k).wait_recv()
        pl.when(has_onward)(lambda: fwd_z(k).start())
        start_line(k, 1)
    for k in (1, 0):
        @pl.when(has_behind)
        def _():
            fwd_z(k).wait_recv()
            start_line(k, 2)

    def finish_halo(k):
        for piece in range(3):
            for side in range(2):
                there = has_line[side]
                if piece == 2:
                    there = there & has_behind
                pl.when(there)(lambda: fwd_line(k, piece, 1 - side).wait_recv())

    shift_x = jnp.minimum(jnp.maximum(corner[0] - (a - 1) * block, 0), block)
    shift_y = jnp.minimum(jnp.maximum(corner[1] - (b - 1) * block, 0), block)

    def aperture(ext, i):
        return ext[shift_x + i, pl.ds(shift_y, width), :]

    def stage_b(rows):
        vz = []
        for i in rows:
            r = 1.0 / aperture(ext_r, i)
            inv[i] = r
            t = -time_ratio * r
            vx1[i + 4] = t * ex[i]
            vy1[i, 8:width + 8, :] = t * ey[i]
            z = t * ez[i]
            vz1[i] = z
            vz.append(z)
        for i, d in zip(rows, along_z(vz, w_minus[...])):
            zd[i] = d

    def stage_c(rows):
        for i in rows:
            v = aperture(ext_v, i)
            k = time_ratio * aperture(ext_r, i) * v * v
            s = dx_minus(vx1, i) + dy_minus(vy1, i) + zd[i]
            kk[i] = k
            s1[i] = s
            put_rows(p1, i, body_rows(p0, i) - k * s)

    def stage_d(rows):
        vz = []
        z = along_z([body_rows(p1, i) for i in rows], w_plus[...])
        for i, dz in zip(rows, z):
            t = -time_ratio * inv[i]
            vx2[i + 4] = vx1[i + 4] + t * dx_plus(p1, i)
            vy2[i, 8:width + 8, :] = vy1[i, 8:width + 8, :] + t * dy_plus(p1, i)
            v = vz1[i] + t * dz
            vz2[i] = v
            vz.append(v)
        for i, d in zip(rows, along_z(vz, w_minus[...])):
            zd[i] = d

    def stage_e(rows):
        for i in rows:
            s = dx_minus(vx2, i) + dy_minus(vy2, i) + zd[i]
            k = kk[i]
            q = body_rows(p1, i) - k * s - obs[i]
            q2[i] = q
            ss[i] = s * q
            put_rows(a2, i, -k * q)

    def stage_f(rows):
        bz = []
        z = along_z([body_rows(a2, i) for i in rows], w_plus[...])
        for i, dz in zip(rows, z):
            r = inv[i]
            dx = dx_plus(a2, i)
            dy = dy_plus(a2, i)
            rr[i] = dx * vx2[i + 4] + dy * vy2[i, 8:width + 8, :] + dz * vz2[i]
            bx[i + 4] = r * dx
            by[i, 8:width + 8, :] = r * dy
            bz.append(r * dz)
        for i, d in zip(rows, along_z(bz, w_minus[...])):
            zd[i] = d

    def stage_g(rows):
        for i in rows:
            q1 = q2[i] - time_ratio * (dx_minus(bx, i) + dy_minus(by, i) + zd[i])
            put_rows(a1, i, -kk[i] * q1)
            s = ss[i] + s1[i] * q1
            ss[i] = s
            grad_v[i + block, block:block + width, :] = (
                -2.0 * time_ratio * aperture(ext_r, i) * aperture(ext_v, i) * s
            )

    def stage_h(rows):
        z = along_z([body_rows(a1, i) for i in rows], w_plus[...])
        for i, dz in zip(rows, z):
            total = rr[i] + dx_plus(a1, i) * vx1[i + 4]
            total = total + dy_plus(a1, i) * vy1[i, 8:width + 8, :] + dz * vz1[i]
            v = aperture(ext_v, i)
            grad_r[i + block, block:block + width, :] = inv[i] * total - time_ratio * v * v * ss[i]

    def back_line(k, slot, side):
        return remote(
            sl.at[k, slot, side], rl.at[k, slot, side], rl_s.at[k, slot, side], rl_r.at[k, slot, side],
            (line_to[side], b),
        )

    def back_z(k):
        return remote(zs.at[k], zr.at[k], rz_s.at[k], rz_r.at[k], (a, behind))

    def back_y(k):
        return remote(ys.at[k], yr.at[k], ry_s.at[k], ry_r.at[k], (a, partner))

    def term(k, slot_x, slot_y, i):
        return grads[k][block + slot_x * block - shift_x + i, pl.ds(block + slot_y * block - shift_y, block), :]

    order = (far, near, 1)

    def send_line(k):
        for slot in order:
            for side in range(2):
                @pl.when(has_line[side])
                def _():
                    def fill(i, carry):
                        sl[k, slot, side, i] = term(k, 2 * side, slot, i)
                        return carry
                    lax.fori_loop(0, block, fill, 0)
                    back_line(k, slot, side).start()

    for side in range(2):
        @pl.when(jnp.logical_not(has_line[side]))
        def _():
            for k in range(2):
                for slot in range(3):
                    rl[k, slot, 1 - side] = jnp.zeros((block, block, depth), jnp.float32)

    @pl.when(jnp.logical_not(has_onward))
    def _():
        for k in range(2):
            zr[k] = jnp.zeros((block, block, depth), jnp.float32)

    finish_halo(1)
    over(stage_b)
    finish_halo(0)
    over(stage_c)
    over(stage_d)
    over(stage_e)
    over(stage_f)
    over(stage_g)
    send_line(0)
    over(stage_h)
    send_line(1)

    def wait_line(k, slot):
        for side in range(2):
            pl.when(has_line[side])(lambda: back_line(k, slot, 1 - side).wait_recv())

    def gather(k, slot, out, extra):
        wait_line(k, slot)
        if extra is not None:
            extra[1]()
        def add(i, carry):
            total = term(k, 1, slot, i) + rl[k, slot, 0, i] + rl[k, slot, 1, i]
            if extra is not None:
                total = total + extra[0][k, i]
            out[i] = total
            return carry
        lax.fori_loop(0, block, add, 0)

    for k in range(2):
        @pl.when(has_behind)
        def _():
            gather(k, far, zs.at[k], None)
            back_z(k).start()
        @pl.when(jnp.logical_not(has_behind))
        def _():
            wait_line(k, far)
    for k in range(2):
        gather(k, near, ys.at[k], (zr, lambda: pl.when(has_onward)(lambda: back_z(k).wait_recv())))
        back_y(k).start()
    for k in range(2):
        gather(k, 1, outs[k], (yr, lambda: back_y(k).wait_recv()))

    for k in range(2):
        fwd_y(k).wait_send()
        back_y(k).wait_send()
        pl.when(has_onward)(lambda: fwd_z(k).wait_send())
        pl.when(has_behind)(lambda: back_z(k).wait_send())
        for side in range(2):
            @pl.when(has_line[side])
            def _():
                for piece in range(2):
                    fwd_line(k, piece, side).wait_send()
                for slot in order:
                    back_line(k, slot, side).wait_send()
            pl.when(has_line[side] & has_behind)(lambda: fwd_line(k, 2, side).wait_send())


def body(n_line, n_shot, velocity, density, start_pressure, observed, corners):
    block, _, depth = velocity.shape
    width = start_pressure.shape[0]
    cells = jax.ShapeDtypeStruct(velocity.shape, jnp.float32)

    def scratch(*shape):
        return pltpu.VMEM(shape, jnp.float32)

    padded = scratch(width + 8, width + 16, depth)
    along_x = scratch(width + 8, width, depth)
    along_y = scratch(width, width + 16, depth)
    plain = scratch(width, width, depth)
    extended = scratch(3 * block, 3 * block, depth)
    wide = scratch(2 * block + width, 2 * block + width, depth)
    matrix = pltpu.VMEM((2 * depth, 2 * depth), jnp.bfloat16)
    pieces = scratch(2, 3, 2, block, block, depth)
    pair = scratch(2, block, block, depth)
    sem = pltpu.SemaphoreType.DMA
    vmem = pl.BlockSpec(memory_space=pltpu.VMEM)
    return pl.pallas_call(
        functools.partial(kernel, n_line, n_shot),
        out_shape=(cells, cells),
        in_specs=[pl.BlockSpec(memory_space=pltpu.SMEM)] + [vmem] * 4,
        out_specs=(vmem, vmem),
        scratch_shapes=[extended] * 2 + [wide] * 2 + [padded] * 4 + [along_x] * 3 + [along_y] * 3
        + [plain] * 13 + [matrix] * 2 + [pieces] * 2 + [pair] * 4
        + [sem((2,))] * 4 + [sem((2, 3, 2))] * 4 + [sem((2,))] * 4,
        compiler_params=pltpu.CompilerParams(
            collective_id=0, has_side_effects=True, vmem_limit_bytes=56 * 1024 * 1024
        ),
    )(corners.reshape(2), velocity, density, start_pressure, observed)


def solution(mesh):
    placed = P("line", "shot", None)
    return jax.shard_map(
        functools.partial(body, mesh.shape["line"], mesh.shape["shot"]),
        mesh=mesh,
        in_specs=(placed,) * 5,
        out_specs=(placed, placed),
        check_vma=False,
    )
```

time: 107 us -> 46 us (0.43)
  the two profiles are of different devices: /device:TPU:9 before, /device:TPU:10 now
where the time goes in v1:
time: 46 us; the launch traced here: 45.9 us
  Pallas kernels  43 us (93%)
  local copies, waits for them, and re-layouts  2.26 us (5%)
  between operations  0.65 us (1%)
    pallas_call x1, Pallas kernels, body(): pl.pallas_call(functools.partial(kernel, n_line, n_shot), out_shape=(cell...  43 us
    unnamed x4, local copies, waits for them, and re-layouts  2.26 us

profile of v1, /device:TPU:10, one launch (start us, length us, event | category | flops | bytes accessed | tf_op | source)
XLA Modules:
  0.0 45.9 jit_solution(9322479379523533536)
XLA Ops:
  0.6 43.0 %shard_map.68 = (f32[16,16,128]{2,1,0:T(8,128)}, f32[16,16,128]{2,1,0:T(8,128)}) custom-call(s32[2]{0:T(128)} %bitcast.1, f32[16,16,128]{2,1,0:T(8,128)} %vel_in.1, f32[16,16,128]{2,1,0:T(8,128)} %rho_in.1, f32[32,32,128]{2,1,0:T(8,128)} %p_in.1, f32[32,32,128]{2,1,0:T(8,128)} %obs_in.1), custom_call_target="tpu_custom_call" | custom-call | tf_op jit(solution)/shard_map/pallas_call | solution.py:428
  43.6 0.0 copy-start
  43.6 1.6 %copy.9 = f32[16,16,128]{2,1,0:T(8,128)} copy(f32[16,16,128]{2,1,0:T(8,128)} %get-tuple-element.4) | data formatting | bytes 262144
  45.2 0.0 copy-done
  45.2 0.7 %copy.10 = f32[16,16,128]{2,1,0:T(8,128)} copy(f32[16,16,128]{2,1,0:T(8,128)S(1)} %copy-done) | data formatting | bytes 262144
Async XLA Ops:
  43.6 1.6 %copy-start = (f32[16,16,128]{2,1,0:T(8,128)S(1)}, f32[16,16,128]{2,1,0:T(8,128)}, u32[]{:S(2)}) copy-start(f32[16,16,128]{2,1,0:T(8,128)} %get-tuple-element.5) | copy-start | bytes 393220

commit v2 on v1

--- a/solution.py
+++ b/solution.py
@@ -14,6 +14,7 @@
 time_ratio = 0.1
 wavelet = (20.0, -12.0)
 RB = 4
+RB_Z = 16
 
 
 def split(value):
@@ -61,7 +62,7 @@
 def kernel(
     n_line, n_shot,
     corner, vel_in, rho_in, p_in, obs_in,
-    vel_out, rho_out,
+    out,
     ext_v, ext_r, grad_v, grad_r,
     p0, p1, a2, a1, vx1, vx2, bx, vy1, vy2, by,
     ex, ey, ez, zd, inv, kk, s1, ss, q2, vz1, vz2, rr, obs, w_plus, w_minus,
@@ -84,7 +85,6 @@
     far = 2 * odd
     exts = (ext_v, ext_r)
     ins = (vel_in, rho_in)
-    outs = (vel_out, rho_out)
     grads = (grad_v, grad_r)
 
     barrier = pltpu.get_barrier_semaphore()
@@ -168,13 +168,11 @@
             return carry
         lax.fori_loop(0, wide, clear_grad, 0)
 
-    steps = width // RB
-
-    def over(step):
+    def over(step, size=RB):
         def body(i, carry):
-            step([i * RB + k for k in range(RB)])
+            step([i * size + k for k in range(size)])
             return carry
-        lax.fori_loop(0, steps, body, 0)
+        lax.fori_loop(0, width // size, body, 0)
 
     def dx_plus(f, i):
         return combine([(f[i + 4 + m, 8:width + 8, :], f[i + 5 - m, 8:width + 8, :]) for m in range(1, 5)])
@@ -201,7 +199,7 @@
             ey[i] = dy_plus(p0, i)
             ez[i] = dz
 
-    over(stage_a)
+    over(stage_a, RB_Z)
     lane = lax.broadcasted_iota(jnp.int32, (1, depth), 1)
     spot = jnp.where(lane == depth // 2, 1.0, 0.0).astype(jnp.float32)
     half = width // 2
@@ -350,15 +348,15 @@
             zr[k] = jnp.zeros((block, block, depth), jnp.float32)
 
     finish_halo(1)
-    over(stage_b)
+    over(stage_b, RB_Z)
     finish_halo(0)
     over(stage_c)
-    over(stage_d)
+    over(stage_d, RB_Z)
     over(stage_e)
-    over(stage_f)
+    over(stage_f, RB_Z)
     over(stage_g)
     send_line(0)
-    over(stage_h)
+    over(stage_h, RB_Z)
     send_line(1)
 
     def wait_line(k, slot):
@@ -389,7 +387,7 @@
         gather(k, near, ys.at[k], (zr, lambda: pl.when(has_onward)(lambda: back_z(k).wait_recv())))
         back_y(k).start()
     for k in range(2):
-        gather(k, 1, outs[k], (yr, lambda: back_y(k).wait_recv()))
+        gather(k, 1, out.at[k], (yr, lambda: back_y(k).wait_recv()))
 
     for k in range(2):
         fwd_y(k).wait_send()
@@ -406,6 +404,11 @@
             pl.when(has_line[side] & has_behind)(lambda: fwd_line(k, 2, side).wait_send())
 
 
+def apart(both, vel_out, rho_out):
+    vel_out[...] = both[0]
+    rho_out[...] = both[1]
+
+
 def body(n_line, n_shot, velocity, density, start_pressure, observed, corners):
     block, _, depth = velocity.shape
     width = start_pressure.shape[0]
@@ -425,11 +428,11 @@
     pair = scratch(2, block, block, depth)
     sem = pltpu.SemaphoreType.DMA
     vmem = pl.BlockSpec(memory_space=pltpu.VMEM)
-    return pl.pallas_call(
+    both = pl.pallas_call(
         functools.partial(kernel, n_line, n_shot),
-        out_shape=(cells, cells),
+        out_shape=jax.ShapeDtypeStruct((2,) + velocity.shape, jnp.float32),
         in_specs=[pl.BlockSpec(memory_space=pltpu.SMEM)] + [vmem] * 4,
-        out_specs=(vmem, vmem),
+        out_specs=vmem,
         scratch_shapes=[extended] * 2 + [wide] * 2 + [padded] * 4 + [along_x] * 3 + [along_y] * 3
         + [plain] * 13 + [matrix] * 2 + [pieces] * 2 + [pair] * 4
         + [sem((2,))] * 4 + [sem((2, 3, 2))] * 4 + [sem((2,))] * 4,
@@ -437,6 +440,9 @@
             collective_id=0, has_side_effects=True, vmem_limit_bytes=56 * 1024 * 1024
         ),
     )(corners.reshape(2), velocity, density, start_pressure, observed)
+    return pl.pallas_call(
+        apart, out_shape=(cells, cells), in_specs=[vmem], out_specs=(vmem, vmem)
+    )(both)
 
 
 def solution(mesh):

time: 46 us -> 42.6 us (0.926)
  the two profiles are of different devices: /device:TPU:10 before, /device:TPU:18 now
where the time goes in v2:
time: 42.6 us; the launch traced here: 42.4 us
  Pallas kernels  41.8 us (98%)
  between operations  0.64 us (2%)
    pallas_call x1, Pallas kernels, body(): pl.pallas_call(functools.partial(kernel, n_line, n_shot), out_shape=jax.S...  40.1 us
    pallas_call x1, Pallas kernels, body(): pl.pallas_call(apart, out_shape=(cells, cells), in_specs=[vmem], out_spec...  1.66 us

profile of v2, /device:TPU:18, one launch (start us, length us, event | category | flops | bytes accessed | tf_op | source)
XLA Modules:
  0.0 42.4 jit_solution(6810077359633949994)
XLA Ops:
  0.6 40.1 %shard_map.68.both = f32[2,16,16,128]{3,2,1,0:T(8,128)} custom-call(s32[2]{0:T(128)} %bitcast.1, f32[16,16,128]{2,1,0:T(8,128)} %vel_in.1, f32[16,16,128]{2,1,0:T(8,128)} %rho_in.1, f32[32,32,128]{2,1,0:T(8,128)} %p_in.1, f32[32,32,128]{2,1,0:T(8,128)} %obs_in.1), custom_call_target="tpu_custom_call" | custom-call | tf_op jit(solution)/shard_map/pallas_call | solution.py:431
  40.8 1.7 %shard_map.69 = (f32[16,16,128]{2,1,0:T(8,128)}, f32[16,16,128]{2,1,0:T(8,128)}) custom-call(f32[2,16,16,128]{3,2,1,0:T(8,128)} %shard_map.68.both), custom_call_target="tpu_custom_call" | custom-call | tf_op jit(solution)/shard_map/pallas_call | solution.py:443

commit v3 on v2

--- a/solution.py
+++ b/solution.py
@@ -65,7 +65,7 @@
     out,
     ext_v, ext_r, grad_v, grad_r,
     p0, p1, a2, a1, vx1, vx2, bx, vy1, vy2, by,
-    ex, ey, ez, zd, inv, kk, s1, ss, q2, vz1, vz2, rr, obs, w_plus, w_minus,
+    ex, ey, ez, zd, inv, kk, s1, ss, q2, vz1, vz2, rr, obs, dens, speed, w_plus, w_minus,
     sl, rl, zs, zr, ys, yr,
     fy_s, fy_r, fz_s, fz_r, fl_s, fl_r, rl_s, rl_r, rz_s, rz_r, ry_s, ry_r,
 ):
@@ -142,23 +142,19 @@
 
     for k in range(2):
         exts[k][block:2 * block, block:2 * block, :] = ins[k][...]
-    for field in (p0, p1, a2, a1):
-        field[0:4, :, :] = jnp.zeros((4, width + 16, depth), jnp.float32)
-        field[width + 4:width + 8, :, :] = jnp.zeros((4, width + 16, depth), jnp.float32)
-    for field in (vx1, vx2, bx):
+    for field in (p0, p1, a2, a1, vx1, vx2, bx):
         field[0:4, :, :] = jnp.zeros((4, width, depth), jnp.float32)
         field[width + 4:width + 8, :, :] = jnp.zeros((4, width, depth), jnp.float32)
 
-    def clear(i, carry):
-        nothing = jnp.zeros((8, depth), jnp.float32)
-        for field, at in ((p0, 4), (p1, 4), (a2, 4), (a1, 4), (vy1, 0), (vy2, 0), (by, 0)):
-            field[i + at, 0:8, :] = nothing
-            field[i + at, width + 8:width + 16, :] = nothing
-        p0[i + 4, 8:width + 8, :] = p_in[i]
-        obs[i] = obs_in[i]
+    turns = width // 8
+
+    def reorder(i, carry):
+        for t in range(turns):
+            p0[i + 4, 8 * t:8 * t + 8, :] = p_in[i, pl.ds(t, 8, turns), :]
+            obs[i, 8 * t:8 * t + 8, :] = obs_in[i, pl.ds(t, 8, turns), :]
         return carry
 
-    lax.fori_loop(0, width, clear, 0)
+    lax.fori_loop(0, width, reorder, 0)
     w_plus[...] = band(depth, True)
     w_minus[...] = band(depth, False)
     wide = 2 * block + width
@@ -174,26 +170,36 @@
             return carry
         lax.fori_loop(0, width // size, body, 0)
 
+    sub = lax.broadcasted_iota(jnp.int32, (8, depth), 0)
+
+    def reach(row):
+        f = [row[8 * t:8 * t + 8] for t in range(turns)]
+        down = [jnp.where(sub == 0, 0.0, pltpu.roll(x, 1, 0)) for x in f]
+        up = [jnp.where(sub == 7, 0.0, pltpu.roll(x, 7, 0)) for x in f]
+        return down + f + up
+
     def dx_plus(f, i):
-        return combine([(f[i + 4 + m, 8:width + 8, :], f[i + 5 - m, 8:width + 8, :]) for m in range(1, 5)])
+        return combine([(f[i + 4 + m], f[i + 5 - m]) for m in range(1, 5)])
 
     def dy_plus(f, i):
-        return combine([(f[i + 4, 8 + m:width + 8 + m, :], f[i + 4, 9 - m:width + 9 - m, :]) for m in range(1, 5)])
-
-    def dx_minus(f, i):
-        return combine([(f[i + 3 + m], f[i + 4 - m]) for m in range(1, 5)])
-
-    def dy_minus(f, i):
-        return combine([(f[i, 7 + m:width + 7 + m, :], f[i, 8 - m:width + 8 - m, :]) for m in range(1, 5)])
-
-    def body_rows(f, i):
-        return f[i + 4, 8:width + 8, :]
-
-    def put_rows(f, i, value):
-        f[i + 4, 8:width + 8, :] = value
+        near_by = reach(f[i + 4])
+        parts = []
+        for t in range(turns, 2 * turns):
+            parts.append(combine([(near_by[t + m], near_by[t + 1 - m]) for m in range(1, 5)]))
+        return jnp.concatenate(parts, axis=0)
+
+    def dxy_minus(fx, fy, i):
+        near_by = reach(fy[i])
+        total = None
+        for m in range(1, 5):
+            gap = fx[i + 3 + m] - fx[i + 4 - m]
+            side = [near_by[t + m - 1] - near_by[t - m] for t in range(turns, 2 * turns)]
+            term = coeffs[m - 1] * (gap + jnp.concatenate(side, axis=0))
+            total = term if total is None else total + term
+        return total
 
     def stage_a(rows):
-        z = along_z([p_in[i] for i in rows], w_plus[...])
+        z = along_z([p0[i + 4] for i in rows], w_plus[...])
         for i, dz in zip(rows, z):
             ex[i] = dx_plus(p0, i)
             ey[i] = dy_plus(p0, i)
@@ -203,8 +209,9 @@
     lane = lax.broadcasted_iota(jnp.int32, (1, depth), 1)
     spot = jnp.where(lane == depth // 2, 1.0, 0.0).astype(jnp.float32)
     half = width // 2
-    p0[half + 4, half + 8:half + 9, :] = p0[half + 4, half + 8:half + 9, :] + wavelet[0] * spot
-    obs[half, half:half + 1, :] = obs[half, half:half + 1, :] - wavelet[1] * spot
+    at = 8 * (half % turns) + half // turns
+    p0[half + 4, at:at + 1, :] = p0[half + 4, at:at + 1, :] + wavelet[0] * spot
+    obs[half, at:at + 1, :] = obs[half, at:at + 1, :] - wavelet[1] * spot
 
     for k in (1, 0):
         fwd_y(k).wait_recv()
@@ -228,16 +235,23 @@
     shift_y = jnp.minimum(jnp.maximum(corner[1] - (b - 1) * block, 0), block)
 
     def aperture(ext, i):
-        return ext[shift_x + i, pl.ds(shift_y, width), :]
+        parts = [ext[shift_x + i, pl.ds(shift_y + t, 8, turns), :] for t in range(turns)]
+        return jnp.concatenate(parts, axis=0)
+
+    def put_grad(grad, i, value):
+        for t in range(turns):
+            grad[i + block, pl.ds(block + t, 8, turns), :] = value[8 * t:8 * t + 8]
 
     def stage_b(rows):
         vz = []
         for i in rows:
-            r = 1.0 / aperture(ext_r, i)
+            rho = aperture(ext_r, i)
+            r = 1.0 / rho
+            dens[i] = rho
             inv[i] = r
             t = -time_ratio * r
             vx1[i + 4] = t * ex[i]
-            vy1[i, 8:width + 8, :] = t * ey[i]
+            vy1[i] = t * ey[i]
             z = t * ez[i]
             vz1[i] = z
             vz.append(z)
@@ -247,19 +261,20 @@
     def stage_c(rows):
         for i in rows:
             v = aperture(ext_v, i)
-            k = time_ratio * aperture(ext_r, i) * v * v
-            s = dx_minus(vx1, i) + dy_minus(vy1, i) + zd[i]
+            k = time_ratio * dens[i] * v * v
+            speed[i] = v
+            s = dxy_minus(vx1, vy1, i) + zd[i]
             kk[i] = k
             s1[i] = s
-            put_rows(p1, i, body_rows(p0, i) - k * s)
+            p1[i + 4] = p0[i + 4] - k * s
 
     def stage_d(rows):
         vz = []
-        z = along_z([body_rows(p1, i) for i in rows], w_plus[...])
+        z = along_z([p1[i + 4] for i in rows], w_plus[...])
         for i, dz in zip(rows, z):
             t = -time_ratio * inv[i]
             vx2[i + 4] = vx1[i + 4] + t * dx_plus(p1, i)
-            vy2[i, 8:width + 8, :] = vy1[i, 8:width + 8, :] + t * dy_plus(p1, i)
+            vy2[i] = vy1[i] + t * dy_plus(p1, i)
             v = vz1[i] + t * dz
             vz2[i] = v
             vz.append(v)
@@ -268,44 +283,42 @@
 
     def stage_e(rows):
         for i in rows:
-            s = dx_minus(vx2, i) + dy_minus(vy2, i) + zd[i]
+            s = dxy_minus(vx2, vy2, i) + zd[i]
             k = kk[i]
-            q = body_rows(p1, i) - k * s - obs[i]
+            q = p1[i + 4] - k * s - obs[i]
             q2[i] = q
             ss[i] = s * q
-            put_rows(a2, i, -k * q)
+            a2[i + 4] = -k * q
 
     def stage_f(rows):
         bz = []
-        z = along_z([body_rows(a2, i) for i in rows], w_plus[...])
+        z = along_z([a2[i + 4] for i in rows], w_plus[...])
         for i, dz in zip(rows, z):
             r = inv[i]
             dx = dx_plus(a2, i)
             dy = dy_plus(a2, i)
-            rr[i] = dx * vx2[i + 4] + dy * vy2[i, 8:width + 8, :] + dz * vz2[i]
+            rr[i] = dx * vx2[i + 4] + dy * vy2[i] + dz * vz2[i]
             bx[i + 4] = r * dx
-            by[i, 8:width + 8, :] = r * dy
+            by[i] = r * dy
             bz.append(r * dz)
         for i, d in zip(rows, along_z(bz, w_minus[...])):
             zd[i] = d
 
     def stage_g(rows):
         for i in rows:
-            q1 = q2[i] - time_ratio * (dx_minus(bx, i) + dy_minus(by, i) + zd[i])
-            put_rows(a1, i, -kk[i] * q1)
+            q1 = q2[i] - time_ratio * (dxy_minus(bx, by, i) + zd[i])
+            a1[i + 4] = -kk[i] * q1
             s = ss[i] + s1[i] * q1
             ss[i] = s
-            grad_v[i + block, block:block + width, :] = (
-                -2.0 * time_ratio * aperture(ext_r, i) * aperture(ext_v, i) * s
-            )
+            put_grad(grad_v, i, -2.0 * time_ratio * dens[i] * speed[i] * s)
 
     def stage_h(rows):
-        z = along_z([body_rows(a1, i) for i in rows], w_plus[...])
+        z = along_z([a1[i + 4] for i in rows], w_plus[...])
         for i, dz in zip(rows, z):
             total = rr[i] + dx_plus(a1, i) * vx1[i + 4]
-            total = total + dy_plus(a1, i) * vy1[i, 8:width + 8, :] + dz * vz1[i]
-            v = aperture(ext_v, i)
-            grad_r[i + block, block:block + width, :] = inv[i] * total - time_ratio * v * v * ss[i]
+            total = total + dy_plus(a1, i) * vy1[i] + dz * vz1[i]
+            v = speed[i]
+            put_grad(grad_r, i, inv[i] * total - time_ratio * v * v * ss[i])
 
     def back_line(k, slot, side):
         return remote(
@@ -417,9 +430,7 @@
     def scratch(*shape):
         return pltpu.VMEM(shape, jnp.float32)
 
-    padded = scratch(width + 8, width + 16, depth)
     along_x = scratch(width + 8, width, depth)
-    along_y = scratch(width, width + 16, depth)
     plain = scratch(width, width, depth)
     extended = scratch(3 * block, 3 * block, depth)
     wide = scratch(2 * block + width, 2 * block + width, depth)
@@ -433,8 +444,8 @@
         out_shape=jax.ShapeDtypeStruct((2,) + velocity.shape, jnp.float32),
         in_specs=[pl.BlockSpec(memory_space=pltpu.SMEM)] + [vmem] * 4,
         out_specs=vmem,
-        scratch_shapes=[extended] * 2 + [wide] * 2 + [padded] * 4 + [along_x] * 3 + [along_y] * 3
-        + [plain] * 13 + [matrix] * 2 + [pieces] * 2 + [pair] * 4
+        scratch_shapes=[extended] * 2 + [wide] * 2 + [along_x] * 7 + [plain] * 18
+        + [matrix] * 2 + [pieces] * 2 + [pair] * 4
         + [sem((2,))] * 4 + [sem((2, 3, 2))] * 4 + [sem((2,))] * 4,
         compiler_params=pltpu.CompilerParams(
             collective_id=0, has_side_effects=True, vmem_limit_bytes=56 * 1024 * 1024

time: 42.6 us -> 42.4 us (level)
  the two profiles are of different devices: /device:TPU:18 before, /device:TPU:10 now
where the time goes in v3:
time: 42.4 us; the launch traced here: 42.2 us
  Pallas kernels  41.6 us (98%)
  between operations  0.64 us (2%)
    pallas_call x1, Pallas kernels, body(): pl.pallas_call(functools.partial(kernel, n_line, n_shot), out_shape=jax.S...  39.9 us
    pallas_call x1, Pallas kernels, body(): pl.pallas_call(apart, out_shape=(cells, cells), in_specs=[vmem], out_spec...  1.66 us

profile of v3, /device:TPU:10, one launch (start us, length us, event | category | flops | bytes accessed | tf_op | source)
XLA Modules:
  0.0 42.2 jit_solution(15784294344996993485)
XLA Ops:
  0.6 39.9 %shard_map.68.both = f32[2,16,16,128]{3,2,1,0:T(8,128)} custom-call(s32[2]{0:T(128)} %bitcast.1, f32[16,16,128]{2,1,0:T(8,128)} %vel_in.1, f32[16,16,128]{2,1,0:T(8,128)} %rho_in.1, f32[32,32,128]{2,1,0:T(8,128)} %p_in.1, f32[32,32,128]{2,1,0:T(8,128)} %obs_in.1), custom_call_target="tpu_custom_call" | custom-call | tf_op jit(solution)/shard_map/pallas_call | solution.py:442
  40.5 1.7 %shard_map.69 = (f32[16,16,128]{2,1,0:T(8,128)}, f32[16,16,128]{2,1,0:T(8,128)}) custom-call(f32[2,16,16,128]{3,2,1,0:T(8,128)} %shard_map.68.both), custom_call_target="tpu_custom_call" | custom-call | tf_op jit(solution)/shard_map/pallas_call | solution.py:454

commit v4 on v3

--- a/solution.py
+++ b/solution.py
@@ -13,6 +13,7 @@
 coeffs = (1225.0 / 1024.0, -245.0 / 3072.0, 49.0 / 5120.0, -5.0 / 7168.0)
 time_ratio = 0.1
 wavelet = (20.0, -12.0)
+PARTS = 2
 RB = 4
 RB_Z = 16
 
@@ -79,8 +80,11 @@
     behind = b - 2 + 4 * odd
     has_onward = (onward >= 0) & (onward < n_shot)
     has_behind = (behind >= 0) & (behind < n_shot)
-    line_to = (a - 1, a + 1)
     has_line = (a > 0, a < n_line - 1)
+    rows_of = block // PARTS
+    chunks = [(k, h) for k in (1, 0) for h in range(PARTS)]
+    back_chunks = [(k, h) for k in (0, 1) for h in range(PARTS)]
+    sides = (lax.rem(a, 2), 1 - lax.rem(a, 2))
     near = 2 * (1 - odd)
     far = 2 * odd
     exts = (ext_v, ext_r)
@@ -107,7 +111,12 @@
     def cols(slot):
         return pl.ds(pl.multiple_of(slot * block, block), block)
 
-    mid = pl.ds(block, block)
+    def to_side(side):
+        there = a - 1 + 2 * side
+        return there, (there >= 0) & (there < n_line)
+
+    def part(h, base=0):
+        return pl.ds(base + h * rows_of, rows_of)
 
     def remote(src, dst, send, recv, there):
         return pltpu.make_async_remote_copy(
@@ -115,30 +124,33 @@
             device_id=there, device_id_type=MESH,
         )
 
-    def fwd_y(k):
-        return remote(ins[k], exts[k].at[mid, cols(far), :], fy_s.at[k], fy_r.at[k], (a, partner))
-
-    def fwd_z(k):
+    def fwd_y(k, h):
         return remote(
-            exts[k].at[mid, cols(near), :], exts[k].at[mid, cols(far), :],
-            fz_s.at[k], fz_r.at[k], (a, onward),
+            ins[k].at[part(h)], exts[k].at[part(h, block), cols(far), :],
+            fy_s.at[k, h], fy_r.at[k, h], (a, partner),
         )
 
-    def fwd_line(k, piece, side):
+    def fwd_z(k, h):
+        return remote(
+            exts[k].at[part(h, block), cols(near), :], exts[k].at[part(h, block), cols(far), :],
+            fz_s.at[k, h], fz_r.at[k, h], (a, onward),
+        )
+
+    def fwd_line(k, h, piece, side):
         slot = (1, near, far)[piece]
-        src = ins[k] if piece == 0 else exts[k].at[mid, cols(slot), :]
-        dst = exts[k].at[pl.ds(2 * block * (1 - side), block), cols(slot), :]
+        src = ins[k].at[part(h)] if piece == 0 else exts[k].at[part(h, block), cols(slot), :]
+        dst = exts[k].at[part(h, 2 * block * (1 - side)), cols(slot), :]
         return remote(
-            src, dst, fl_s.at[k, piece, side], fl_r.at[k, piece, side], (line_to[side], b)
+            src, dst, fl_s.at[k, h, piece, side], fl_r.at[k, h, piece, side], (to_side(side)[0], b)
         )
 
-    def start_line(k, piece):
-        for side in range(2):
-            pl.when(has_line[side])(lambda side=side: fwd_line(k, piece, side).start())
-
-    for k in (1, 0):
-        fwd_y(k).start()
-        start_line(k, 0)
+    def start_line(k, h, piece):
+        for side in sides:
+            pl.when(to_side(side)[1])(lambda: fwd_line(k, h, piece, side).start())
+
+    for k, h in chunks:
+        fwd_y(k, h).start()
+        start_line(k, h, 0)
 
     for k in range(2):
         exts[k][block:2 * block, block:2 * block, :] = ins[k][...]
@@ -158,17 +170,18 @@
     w_plus[...] = band(depth, True)
     w_minus[...] = band(depth, False)
     wide = 2 * block + width
-    for grad in grads:
-        def clear_grad(i, carry, grad=grad):
-            grad[i] = jnp.zeros((wide, depth), jnp.float32)
+
+    def clear_grad(k):
+        def clear(i, carry):
+            grads[k][i] = jnp.zeros((wide, depth), jnp.float32)
             return carry
-        lax.fori_loop(0, wide, clear_grad, 0)
-
-    def over(step, size=RB):
+        lax.fori_loop(0, wide, clear, 0)
+
+    def over(step, size=RB, first=0, last=width):
         def body(i, carry):
             step([i * size + k for k in range(size)])
             return carry
-        lax.fori_loop(0, width // size, body, 0)
+        lax.fori_loop(first // size, last // size, body, 0)
 
     sub = lax.broadcasted_iota(jnp.int32, (8, depth), 0)
 
@@ -205,7 +218,30 @@
             ey[i] = dy_plus(p0, i)
             ez[i] = dz
 
-    over(stage_a, RB_Z)
+    def relay_near(k, h):
+        fwd_y(k, h).wait_recv()
+        pl.when(has_onward)(lambda: fwd_z(k, h).start())
+        start_line(k, h, 1)
+
+    def relay_far(k, h):
+        @pl.when(has_behind)
+        def _():
+            fwd_z(k, h).wait_recv()
+            start_line(k, h, 2)
+
+    for h in range(PARTS):
+        relay_near(1, h)
+        if h % (PARTS // 2) == 0:
+            at = h // (PARTS // 2) * (width // 2)
+            over(stage_a, RB_Z, at, at + width // 2)
+    for h in range(PARTS):
+        relay_near(0, h)
+        relay_far(1, h)
+        if h % (PARTS // 2) == 0:
+            clear_grad(h // (PARTS // 2))
+    for h in range(PARTS):
+        relay_far(0, h)
+
     lane = lax.broadcasted_iota(jnp.int32, (1, depth), 1)
     spot = jnp.where(lane == depth // 2, 1.0, 0.0).astype(jnp.float32)
     half = width // 2
@@ -213,23 +249,14 @@
     p0[half + 4, at:at + 1, :] = p0[half + 4, at:at + 1, :] + wavelet[0] * spot
     obs[half, at:at + 1, :] = obs[half, at:at + 1, :] - wavelet[1] * spot
 
-    for k in (1, 0):
-        fwd_y(k).wait_recv()
-        pl.when(has_onward)(lambda: fwd_z(k).start())
-        start_line(k, 1)
-    for k in (1, 0):
-        @pl.when(has_behind)
-        def _():
-            fwd_z(k).wait_recv()
-            start_line(k, 2)
-
     def finish_halo(k):
         for piece in range(3):
             for side in range(2):
                 there = has_line[side]
                 if piece == 2:
                     there = there & has_behind
-                pl.when(there)(lambda: fwd_line(k, piece, 1 - side).wait_recv())
+                for h in range(PARTS):
+                    pl.when(there)(lambda: fwd_line(k, h, piece, 1 - side).wait_recv())
 
     shift_x = jnp.minimum(jnp.maximum(corner[0] - (a - 1) * block, 0), block)
     shift_y = jnp.minimum(jnp.maximum(corner[1] - (b - 1) * block, 0), block)
@@ -320,33 +347,32 @@
             v = speed[i]
             put_grad(grad_r, i, inv[i] * total - time_ratio * v * v * ss[i])
 
-    def back_line(k, slot, side):
+    def back_line(k, h, slot, side):
         return remote(
-            sl.at[k, slot, side], rl.at[k, slot, side], rl_s.at[k, slot, side], rl_r.at[k, slot, side],
-            (line_to[side], b),
+            sl.at[k, slot, side, part(h)], rl.at[k, slot, side, part(h)],
+            rl_s.at[k, h, slot, side], rl_r.at[k, h, slot, side], (to_side(side)[0], b),
         )
 
-    def back_z(k):
-        return remote(zs.at[k], zr.at[k], rz_s.at[k], rz_r.at[k], (a, behind))
-
-    def back_y(k):
-        return remote(ys.at[k], yr.at[k], ry_s.at[k], ry_r.at[k], (a, partner))
+    def back_z(k, h):
+        return remote(zs.at[k, part(h)], zr.at[k, part(h)], rz_s.at[k, h], rz_r.at[k, h], (a, behind))
+
+    def back_y(k, h):
+        return remote(ys.at[k, part(h)], yr.at[k, part(h)], ry_s.at[k, h], ry_r.at[k, h], (a, partner))
 
     def term(k, slot_x, slot_y, i):
         return grads[k][block + slot_x * block - shift_x + i, pl.ds(block + slot_y * block - shift_y, block), :]
 
-    order = (far, near, 1)
-
-    def send_line(k):
-        for slot in order:
-            for side in range(2):
-                @pl.when(has_line[side])
-                def _():
-                    def fill(i, carry):
-                        sl[k, slot, side, i] = term(k, 2 * side, slot, i)
-                        return carry
-                    lax.fori_loop(0, block, fill, 0)
-                    back_line(k, slot, side).start()
+    def send_line(k, slots):
+        for slot in slots:
+            for h in range(PARTS):
+                for side in sides:
+                    @pl.when(to_side(side)[1])
+                    def _():
+                        def fill(i, carry):
+                            sl[k, slot, side, i] = term(k, 2 * side, slot, i)
+                            return carry
+                        lax.fori_loop(h * rows_of, (h + 1) * rows_of, fill, 0)
+                        back_line(k, h, slot, side).start()
 
     for side in range(2):
         @pl.when(jnp.logical_not(has_line[side]))
@@ -368,53 +394,55 @@
     over(stage_e)
     over(stage_f, RB_Z)
     over(stage_g)
-    send_line(0)
+    send_line(0, (far, near))
     over(stage_h, RB_Z)
-    send_line(1)
-
-    def wait_line(k, slot):
+    send_line(1, (far, near))
+    send_line(0, (1,))
+    send_line(1, (1,))
+
+    def wait_line(k, h, slot):
         for side in range(2):
-            pl.when(has_line[side])(lambda: back_line(k, slot, 1 - side).wait_recv())
-
-    def gather(k, slot, out, extra):
-        wait_line(k, slot)
+            pl.when(has_line[side])(lambda: back_line(k, h, slot, 1 - side).wait_recv())
+
+    def gather(k, h, slot, out, extra):
+        wait_line(k, h, slot)
         if extra is not None:
             extra[1]()
         def add(i, carry):
             total = term(k, 1, slot, i) + rl[k, slot, 0, i] + rl[k, slot, 1, i]
             if extra is not None:
                 total = total + extra[0][k, i]
-            out[i] = total
+            out[k, i] = total
             return carry
-        lax.fori_loop(0, block, add, 0)
-
-    for k in range(2):
+        lax.fori_loop(h * rows_of, (h + 1) * rows_of, add, 0)
+
+    for k, h in back_chunks:
         @pl.when(has_behind)
         def _():
-            gather(k, far, zs.at[k], None)
-            back_z(k).start()
+            gather(k, h, far, zs, None)
+            back_z(k, h).start()
         @pl.when(jnp.logical_not(has_behind))
         def _():
-            wait_line(k, far)
-    for k in range(2):
-        gather(k, near, ys.at[k], (zr, lambda: pl.when(has_onward)(lambda: back_z(k).wait_recv())))
-        back_y(k).start()
-    for k in range(2):
-        gather(k, 1, out.at[k], (yr, lambda: back_y(k).wait_recv()))
-
-    for k in range(2):
-        fwd_y(k).wait_send()
-        back_y(k).wait_send()
-        pl.when(has_onward)(lambda: fwd_z(k).wait_send())
-        pl.when(has_behind)(lambda: back_z(k).wait_send())
+            wait_line(k, h, far)
+    for k, h in back_chunks:
+        gather(k, h, near, ys, (zr, lambda: pl.when(has_onward)(lambda: back_z(k, h).wait_recv())))
+        back_y(k, h).start()
+    for k, h in back_chunks:
+        gather(k, h, 1, out, (yr, lambda: back_y(k, h).wait_recv()))
+
+    for k, h in chunks:
+        fwd_y(k, h).wait_send()
+        back_y(k, h).wait_send()
+        pl.when(has_onward)(lambda: fwd_z(k, h).wait_send())
+        pl.when(has_behind)(lambda: back_z(k, h).wait_send())
         for side in range(2):
             @pl.when(has_line[side])
             def _():
                 for piece in range(2):
-                    fwd_line(k, piece, side).wait_send()
-                for slot in order:
-                    back_line(k, slot, side).wait_send()
-            pl.when(has_line[side] & has_behind)(lambda: fwd_line(k, 2, side).wait_send())
+                    fwd_line(k, h, piece, side).wait_send()
+                for slot in range(3):
+                    back_line(k, h, slot, side).wait_send()
+            pl.when(has_line[side] & has_behind)(lambda: fwd_line(k, h, 2, side).wait_send())
 
 
 def apart(both, vel_out, rho_out):
@@ -446,7 +474,7 @@
         out_specs=vmem,
         scratch_shapes=[extended] * 2 + [wide] * 2 + [along_x] * 7 + [plain] * 18
         + [matrix] * 2 + [pieces] * 2 + [pair] * 4
-        + [sem((2,))] * 4 + [sem((2, 3, 2))] * 4 + [sem((2,))] * 4,
+        + [sem((2, PARTS))] * 4 + [sem((2, PARTS, 3, 2))] * 4 + [sem((2, PARTS))] * 4,
         compiler_params=pltpu.CompilerParams(
             collective_id=0, has_side_effects=True, vmem_limit_bytes=56 * 1024 * 1024
         ),

time: 42.4 us -> 39.5 us (0.932)
  the two profiles are of different devices: /device:TPU:10 before, /device:TPU:9 now
where the time goes in v4:
time: 39.5 us; the launch traced here: 39.4 us
  Pallas kernels  38.7 us (98%)
  between operations  0.64 us (2%)
    pallas_call x1, Pallas kernels, body(): pl.pallas_call(functools.partial(kernel, n_line, n_shot), out_shape=jax.S...  37.1 us
    pallas_call x1, Pallas kernels, body(): pl.pallas_call(apart, out_shape=(cells, cells), in_specs=[vmem], out_spec...  1.66 us

profile of v4, /device:TPU:9, one launch (start us, length us, event | category | flops | bytes accessed | tf_op | source)
XLA Modules:
  0.0 39.4 jit_solution(2267879498781636290)
XLA Ops:
  0.6 37.1 %shard_map.68.both = f32[2,16,16,128]{3,2,1,0:T(8,128)} custom-call(s32[2]{0:T(128)} %bitcast.1, f32[16,16,128]{2,1,0:T(8,128)} %vel_in.1, f32[16,16,128]{2,1,0:T(8,128)} %rho_in.1, f32[32,32,128]{2,1,0:T(8,128)} %p_in.1, f32[32,32,128]{2,1,0:T(8,128)} %obs_in.1), custom_call_target="tpu_custom_call" | custom-call | tf_op jit(solution)/shard_map/pallas_call | solution.py:470
  37.7 1.7 %shard_map.69 = (f32[16,16,128]{2,1,0:T(8,128)}, f32[16,16,128]{2,1,0:T(8,128)}) custom-call(f32[2,16,16,128]{3,2,1,0:T(8,128)} %shard_map.68.both), custom_call_target="tpu_custom_call" | custom-call | tf_op jit(solution)/shard_map/pallas_call | solution.py:482

commit v5 on v4

--- a/solution.py
+++ b/solution.py
@@ -67,8 +67,8 @@
     ext_v, ext_r, grad_v, grad_r,
     p0, p1, a2, a1, vx1, vx2, bx, vy1, vy2, by,
     ex, ey, ez, zd, inv, kk, s1, ss, q2, vz1, vz2, rr, obs, dens, speed, w_plus, w_minus,
-    sl, rl, zs, zr, ys, yr,
-    fy_s, fy_r, fz_s, fz_r, fl_s, fl_r, rl_s, rl_r, rz_s, rz_r, ry_s, ry_r,
+    cs, sl, rl, zs, zr, ys, yr, place, places,
+    fy_s, fy_r, fz_s, fz_r, fl_s, fl_r, rl_s, rl_r, rz_s, rz_r, ry_s, ry_r, at_s, at_r,
 ):
     block, _, depth = vel_in.shape
     width = p_in.shape[0]
@@ -137,9 +137,8 @@
         )
 
     def fwd_line(k, h, piece, side):
-        slot = (1, near, far)[piece]
-        src = ins[k].at[part(h)] if piece == 0 else exts[k].at[part(h, block), cols(slot), :]
-        dst = exts[k].at[part(h, 2 * block * (1 - side)), cols(slot), :]
+        src = ins[k].at[part(h)] if piece == 0 else cs.at[k, side, part(h)]
+        dst = exts[k].at[part(h, 2 * block * (1 - side)), cols(1 - piece), :]
         return remote(
             src, dst, fl_s.at[k, h, piece, side], fl_r.at[k, h, piece, side], (to_side(side)[0], b)
         )
@@ -147,6 +146,21 @@
     def start_line(k, h, piece):
         for side in sides:
             pl.when(to_side(side)[1])(lambda: fwd_line(k, h, piece, side).start())
+
+    def tell(side):
+        return remote(
+            place, places.at[1 - side], at_s.at[side], at_r.at[1 - side], (to_side(side)[0], b)
+        )
+
+    shift_x = jnp.minimum(jnp.maximum(corner[0] - (a - 1) * block, 0), block)
+    shift_y = jnp.minimum(jnp.maximum(corner[1] - (b - 1) * block, 0), block)
+    place[...] = jnp.zeros((8, depth), jnp.int32) + shift_y
+    for side in range(2):
+        pl.when(has_line[side])(lambda: tell(side).start())
+
+        @pl.when(jnp.logical_not(has_line[side]))
+        def _():
+            places[side] = jnp.zeros((8, depth), jnp.int32)
 
     for k, h in chunks:
         fwd_y(k, h).start()
@@ -221,13 +235,26 @@
     def relay_near(k, h):
         fwd_y(k, h).wait_recv()
         pl.when(has_onward)(lambda: fwd_z(k, h).start())
-        start_line(k, h, 1)
+
+    column = lax.broadcasted_iota(jnp.int32, (8, depth), 0)
 
     def relay_far(k, h):
-        @pl.when(has_behind)
-        def _():
-            fwd_z(k, h).wait_recv()
-            start_line(k, h, 2)
+        pl.when(has_behind)(lambda: fwd_z(k, h).wait_recv())
+        for side in sides:
+            @pl.when(to_side(side)[1])
+            def _():
+                start = places[side]
+                def fill(i, carry):
+                    for c in range(0, block, 8):
+                        left = exts[k][block + i, c:c + 8, :]
+                        right = exts[k][block + i, 2 * block + c:2 * block + c + 8, :]
+                        cs[k, side, i, c:c + 8, :] = jnp.where(column + c >= start, left, right)
+                    return carry
+                lax.fori_loop(h * rows_of, (h + 1) * rows_of, fill, 0)
+                fwd_line(k, h, 1, side).start()
+
+    for side in range(2):
+        pl.when(has_line[side])(lambda: tell(1 - side).wait_recv())
 
     for h in range(PARTS):
         relay_near(1, h)
@@ -250,16 +277,17 @@
     obs[half, at:at + 1, :] = obs[half, at:at + 1, :] - wavelet[1] * spot
 
     def finish_halo(k):
-        for piece in range(3):
-            for side in range(2):
-                there = has_line[side]
-                if piece == 2:
-                    there = there & has_behind
-                for h in range(PARTS):
-                    pl.when(there)(lambda: fwd_line(k, h, piece, 1 - side).wait_recv())
-
-    shift_x = jnp.minimum(jnp.maximum(corner[0] - (a - 1) * block, 0), block)
-    shift_y = jnp.minimum(jnp.maximum(corner[1] - (b - 1) * block, 0), block)
+        for side in range(2):
+            @pl.when(has_line[side])
+            def _():
+                for piece in range(2):
+                    for h in range(PARTS):
+                        fwd_line(k, h, piece, 1 - side).wait_recv()
+                first = 2 * block * side
+                def both(i, carry):
+                    exts[k][first + i, 2 * block:3 * block, :] = exts[k][first + i, 0:block, :]
+                    return carry
+                lax.fori_loop(0, block, both, 0)
 
     def aperture(ext, i):
         parts = [ext[shift_x + i, pl.ds(shift_y + t, 8, turns), :] for t in range(turns)]
@@ -347,10 +375,10 @@
             v = speed[i]
             put_grad(grad_r, i, inv[i] * total - time_ratio * v * v * ss[i])
 
-    def back_line(k, h, slot, side):
+    def back_line(k, h, piece, side):
         return remote(
-            sl.at[k, slot, side, part(h)], rl.at[k, slot, side, part(h)],
-            rl_s.at[k, h, slot, side], rl_r.at[k, h, slot, side], (to_side(side)[0], b),
+            sl.at[k, piece, side, part(h)], rl.at[k, piece, side, part(h)],
+            rl_s.at[k, h, piece, side], rl_r.at[k, h, piece, side], (to_side(side)[0], b),
         )
 
     def back_z(k, h):
@@ -362,24 +390,26 @@
     def term(k, slot_x, slot_y, i):
         return grads[k][block + slot_x * block - shift_x + i, pl.ds(block + slot_y * block - shift_y, block), :]
 
-    def send_line(k, slots):
-        for slot in slots:
-            for h in range(PARTS):
-                for side in sides:
-                    @pl.when(to_side(side)[1])
-                    def _():
-                        def fill(i, carry):
-                            sl[k, slot, side, i] = term(k, 2 * side, slot, i)
-                            return carry
-                        lax.fori_loop(h * rows_of, (h + 1) * rows_of, fill, 0)
-                        back_line(k, h, slot, side).start()
+    def send_line(k, piece):
+        for h in range(PARTS):
+            for side in sides:
+                @pl.when(to_side(side)[1])
+                def _():
+                    def fill(i, carry):
+                        if piece == 0:
+                            sl[k, 0, side, i] = term(k, 2 * side, 1, i)
+                        else:
+                            sl[k, 1, side, i] = term(k, 2 * side, 0, i) + term(k, 2 * side, 2, i)
+                        return carry
+                    lax.fori_loop(h * rows_of, (h + 1) * rows_of, fill, 0)
+                    back_line(k, h, piece, side).start()
 
     for side in range(2):
         @pl.when(jnp.logical_not(has_line[side]))
         def _():
             for k in range(2):
-                for slot in range(3):
-                    rl[k, slot, 1 - side] = jnp.zeros((block, block, depth), jnp.float32)
+                for piece in range(2):
+                    rl[k, piece, 1 - side] = jnp.zeros((block, block, depth), jnp.float32)
 
     @pl.when(jnp.logical_not(has_onward))
     def _():
@@ -394,41 +424,49 @@
     over(stage_e)
     over(stage_f, RB_Z)
     over(stage_g)
-    send_line(0, (far, near))
+    send_line(0, 1)
     over(stage_h, RB_Z)
-    send_line(1, (far, near))
-    send_line(0, (1,))
-    send_line(1, (1,))
-
-    def wait_line(k, h, slot):
+    send_line(1, 1)
+    send_line(0, 0)
+    send_line(1, 0)
+
+    def wait_line(k, h, piece):
         for side in range(2):
-            pl.when(has_line[side])(lambda: back_line(k, h, slot, 1 - side).wait_recv())
+            pl.when(has_line[side])(lambda: back_line(k, h, piece, 1 - side).wait_recv())
 
     def gather(k, h, slot, out, extra):
-        wait_line(k, h, slot)
-        if extra is not None:
-            extra[1]()
         def add(i, carry):
-            total = term(k, 1, slot, i) + rl[k, slot, 0, i] + rl[k, slot, 1, i]
-            if extra is not None:
-                total = total + extra[0][k, i]
-            out[k, i] = total
+            for c in range(0, block, 8):
+                cells = pl.ds(c, 8)
+                total = grads[k][
+                    2 * block - shift_x + i, pl.ds(block + slot * block - shift_y + c, 8), :
+                ]
+                for side in range(2):
+                    if isinstance(slot, int):
+                        total = total + rl[k, 0, 1 - side, i, cells, :]
+                    else:
+                        inside = (column + c - places[side]) * (1 - slot) - slot // 2 >= 0
+                        total = total + jnp.where(inside, rl[k, 1, 1 - side, i, cells, :], 0.0)
+                if extra is not None:
+                    total = total + extra[k, i, cells, :]
+                out[k, i, cells, :] = total
             return carry
         lax.fori_loop(h * rows_of, (h + 1) * rows_of, add, 0)
 
     for k, h in back_chunks:
+        wait_line(k, h, 1)
         @pl.when(has_behind)
         def _():
             gather(k, h, far, zs, None)
             back_z(k, h).start()
-        @pl.when(jnp.logical_not(has_behind))
-        def _():
-            wait_line(k, h, far)
     for k, h in back_chunks:
-        gather(k, h, near, ys, (zr, lambda: pl.when(has_onward)(lambda: back_z(k, h).wait_recv())))
+        pl.when(has_onward)(lambda: back_z(k, h).wait_recv())
+        gather(k, h, near, ys, zr)
         back_y(k, h).start()
     for k, h in back_chunks:
-        gather(k, h, 1, out, (yr, lambda: back_y(k, h).wait_recv()))
+        wait_line(k, h, 0)
+        back_y(k, h).wait_recv()
+        gather(k, h, 1, out, yr)
 
     for k, h in chunks:
         fwd_y(k, h).wait_send()
@@ -440,9 +478,9 @@
             def _():
                 for piece in range(2):
                     fwd_line(k, h, piece, side).wait_send()
-                for slot in range(3):
-                    back_line(k, h, slot, side).wait_send()
-            pl.when(has_line[side] & has_behind)(lambda: fwd_line(k, h, 2, side).wait_send())
+                    back_line(k, h, piece, side).wait_send()
+    for side in range(2):
+        pl.when(has_line[side])(lambda: tell(side).wait_send())
 
 
 def apart(both, vel_out, rho_out):
@@ -463,7 +501,9 @@
     extended = scratch(3 * block, 3 * block, depth)
     wide = scratch(2 * block + width, 2 * block + width, depth)
     matrix = pltpu.VMEM((2 * depth, 2 * depth), jnp.bfloat16)
-    pieces = scratch(2, 3, 2, block, block, depth)
+    pieces = scratch(2, 2, 2, block, block, depth)
+    place = pltpu.VMEM((8, depth), jnp.int32)
+    places = pltpu.VMEM((2, 8, depth), jnp.int32)
     pair = scratch(2, block, block, depth)
     sem = pltpu.SemaphoreType.DMA
     vmem = pl.BlockSpec(memory_space=pltpu.VMEM)
@@ -473,8 +513,8 @@
         in_specs=[pl.BlockSpec(memory_space=pltpu.SMEM)] + [vmem] * 4,
         out_specs=vmem,
         scratch_shapes=[extended] * 2 + [wide] * 2 + [along_x] * 7 + [plain] * 18
-        + [matrix] * 2 + [pieces] * 2 + [pair] * 4
-        + [sem((2, PARTS))] * 4 + [sem((2, PARTS, 3, 2))] * 4 + [sem((2, PARTS))] * 4,
+        + [matrix] * 2 + [scratch(2, 2, block, block, depth)] + [pieces] * 2 + [pair] * 4 + [place, places]
+        + [sem((2, PARTS))] * 4 + [sem((2, PARTS, 2, 2))] * 4 + [sem((2, PARTS))] * 4 + [sem((2,))] * 2,
         compiler_params=pltpu.CompilerParams(
             collective_id=0, has_side_effects=True, vmem_limit_bytes=56 * 1024 * 1024
         ),

time: 39.5 us -> 39.5 us (level)
  no operation moved by 1% of the time
where the time goes in v5:
time: 39.5 us; the launch traced here: 39.4 us
  Pallas kernels  38.7 us (98%)
  between operations  0.64 us (2%)
    pallas_call x1, Pallas kernels, body(): pl.pallas_call(functools.partial(kernel, n_line, n_shot), out_shape=jax.S...  37.1 us
    pallas_call x1, Pallas kernels, body(): pl.pallas_call(apart, out_shape=(cells, cells), in_specs=[vmem], out_spec...  1.66 us

profile of v5, /device:TPU:9, one launch (start us, length us, event | category | flops | bytes accessed | tf_op | source)
XLA Modules:
  0.0 39.4 jit_solution(7365012047314855196)
XLA Ops:
  0.6 37.1 %shard_map.68.both = f32[2,16,16,128]{3,2,1,0:T(8,128)} custom-call(s32[2]{0:T(128)} %bitcast.1, f32[16,16,128]{2,1,0:T(8,128)} %vel_in.1, f32[16,16,128]{2,1,0:T(8,128)} %rho_in.1, f32[32,32,128]{2,1,0:T(8,128)} %p_in.1, f32[32,32,128]{2,1,0:T(8,128)} %obs_in.1), custom_call_target="tpu_custom_call" | custom-call | tf_op jit(solution)/shard_map/pallas_call | solution.py:510
  37.7 1.7 %shard_map.69 = (f32[16,16,128]{2,1,0:T(8,128)}, f32[16,16,128]{2,1,0:T(8,128)}) custom-call(f32[2,16,16,128]{3,2,1,0:T(8,128)} %shard_map.68.both), custom_call_target="tpu_custom_call" | custom-call | tf_op jit(solution)/shard_map/pallas_call | solution.py:522

commit v6 on v5

--- a/solution.py
+++ b/solution.py
@@ -13,7 +13,7 @@
 coeffs = (1225.0 / 1024.0, -245.0 / 3072.0, 49.0 / 5120.0, -5.0 / 7168.0)
 time_ratio = 0.1
 wavelet = (20.0, -12.0)
-PARTS = 2
+PARTS = 4
 RB = 4
 RB_Z = 16
 
@@ -516,7 +516,7 @@
         + [matrix] * 2 + [scratch(2, 2, block, block, depth)] + [pieces] * 2 + [pair] * 4 + [place, places]
         + [sem((2, PARTS))] * 4 + [sem((2, PARTS, 2, 2))] * 4 + [sem((2, PARTS))] * 4 + [sem((2,))] * 2,
         compiler_params=pltpu.CompilerParams(
-            collective_id=0, has_side_effects=True, vmem_limit_bytes=56 * 1024 * 1024
+            collective_id=0, has_side_effects=True, vmem_limit_bytes=36 * 1024 * 1024
         ),
     )(corners.reshape(2), velocity, density, start_pressure, observed)
     return pl.pallas_call(

time: 39.5 us -> 42.9 us (1.086)
  local copies, waits for them, and re-layouts: 0 us -> 5.23 us
  Pallas kernels: 38.7 us -> 36.5 us
    unnamed x0 -> x12, local copies, waits for them, and re-layouts: none -> 5.23 us
    pallas_call x1, Pallas kernels: 37.1 us -> 34.8 us  [body(): pl.pallas_call(functools.partial(kernel, n_line, n_shot), out_shape=jax.S...]
where the time goes in v6:
time: 42.9 us; the launch traced here: 42.4 us
  Pallas kernels  36.5 us (85%)
  local copies, waits for them, and re-layouts  5.23 us (12%)
  between operations  0.66 us (2%)
    pallas_call x1, Pallas kernels, body(): pl.pallas_call(functools.partial(kernel, n_line, n_shot), out_shape=jax.S...  34.8 us
    unnamed x12, local copies, waits for them, and re-layouts  5.23 us
    pallas_call x1, Pallas kernels, body(): pl.pallas_call(apart, out_shape=(cells, cells), in_specs=[vmem], out_spec...  1.66 us

profile of v6, /device:TPU:9, one launch (start us, length us, event | category | flops | bytes accessed | tf_op | source)
XLA Modules:
  0.0 42.4 jit_solution(4276447018698096889)
XLA Ops:
  0.6 0.0 copy-start.5
  0.6 0.6 %copy-done.5 = s32[1,1,2]{2,1,0:T(1,128)S(1)} copy-done((s32[1,1,2]{2,1,0:T(1,128)S(1)}, s32[1,1,2]{2,1,0:T(1,128)}, u32[]{:S(2)}) %copy-start.5) | copy-done | bytes 32
  1.3 0.0 copy-start.1
  1.3 1.0 %copy-done.1 = f32[32,32,128]{2,1,0:T(8,128)S(1)} copy-done((f32[32,32,128]{2,1,0:T(8,128)S(1)}, f32[32,32,128]{2,1,0:T(8,128)}, u32[]{:S(2)}) %copy-start.1) | copy-done | bytes 524312
  2.3 0.0 copy-start.2
  2.3 1.0 %copy-done.2 = f32[32,32,128]{2,1,0:T(8,128)S(1)} copy-done((f32[32,32,128]{2,1,0:T(8,128)S(1)}, f32[32,32,128]{2,1,0:T(8,128)}, u32[]{:S(2)}) %copy-start.2) | copy-done | bytes 524312
  3.4 0.0 copy-start.3
  3.4 0.9 %copy-done.3 = f32[16,16,128]{2,1,0:T(8,128)S(1)} copy-done((f32[16,16,128]{2,1,0:T(8,128)S(1)}, f32[16,16,128]{2,1,0:T(8,128)}, u32[]{:S(2)}) %copy-start.3) | copy-done | bytes 131096
  4.3 0.0 copy-start.4
  4.3 0.9 %copy-done.4 = f32[16,16,128]{2,1,0:T(8,128)S(1)} copy-done((f32[16,16,128]{2,1,0:T(8,128)S(1)}, f32[16,16,128]{2,1,0:T(8,128)}, u32[]{:S(2)}) %copy-start.4) | copy-done | bytes 131096
  5.2 34.8 %shard_map.68.both = f32[2,16,16,128]{3,2,1,0:T(8,128)S(1)} custom-call(s32[2]{0:T(128)S(1)} %bitcast.1, f32[16,16,128]{2,1,0:T(8,128)S(1)} %copy-done.3, f32[16,16,128]{2,1,0:T(8,128)S(1)} %copy-done.4, f32[32,32,128]{2,1,0:T(8,128)S(1)} %copy-done.1, f32[32,32,128]{2,1,0:T(8,128)S(1)} %copy-done.2), custom_call_target="tpu_custom_call" | custom-call | tf_op jit(solution)/shard_map/pallas_call | solution.py:510
  40.0 0.0 copy-start
  40.0 0.7 %copy-done = f32[2,16,16,128]{3,2,1,0:T(8,128)} copy-done((f32[2,16,16,128]{3,2,1,0:T(8,128)}, f32[2,16,16,128]{3,2,1,0:T(8,128)S(1)}, u32[]{:S(2)}) %copy-start) | copy-done | bytes 262168
  40.7 1.7 %shard_map.69 = (f32[16,16,128]{2,1,0:T(8,128)}, f32[16,16,128]{2,1,0:T(8,128)}) custom-call(f32[2,16,16,128]{3,2,1,0:T(8,128)} %copy-done), custom_call_target="tpu_custom_call" | custom-call | tf_op jit(solution)/shard_map/pallas_call | solution.py:522
Async XLA Ops:
  0.6 0.7 %copy-start.5 = (s32[1,1,2]{2,1,0:T(1,128)S(1)}, s32[1,1,2]{2,1,0:T(1,128)}, u32[]{:S(2)}) copy-start(s32[1,1,2]{2,1,0:T(1,128)} %param.9) | copy-start | bytes 28
  1.3 1.0 %copy-start.1 = (f32[32,32,128]{2,1,0:T(8,128)S(1)}, f32[32,32,128]{2,1,0:T(8,128)}, u32[]{:S(2)}) copy-start(f32[32,32,128]{2,1,0:T(8,128)} %p_in.1) | copy-start | bytes 1572868
  2.3 1.0 %copy-start.2 = (f32[32,32,128]{2,1,0:T(8,128)S(1)}, f32[32,32,128]{2,1,0:T(8,128)}, u32[]{:S(2)}) copy-start(f32[32,32,128]{2,1,0:T(8,128)} %obs_in.1) | copy-start | bytes 1572868
  3.4 0.9 %copy-start.3 = (f32[16,16,128]{2,1,0:T(8,128)S(1)}, f32[16,16,128]{2,1,0:T(8,128)}, u32[]{:S(2)}) copy-start(f32[16,16,128]{2,1,0:T(8,128)} %vel_in.1) | copy-start | bytes 393220
  4.3 0.9 %copy-start.4 = (f32[16,16,128]{2,1,0:T(8,128)S(1)}, f32[16,16,128]{2,1,0:T(8,128)}, u32[]{:S(2)}) copy-start(f32[16,16,128]{2,1,0:T(8,128)} %rho_in.1) | copy-start | bytes 393220
  40.0 0.7 %copy-start = (f32[2,16,16,128]{3,2,1,0:T(8,128)}, f32[2,16,16,128]{3,2,1,0:T(8,128)S(1)}, u32[]{:S(2)}) copy-start(f32[2,16,16,128]{3,2,1,0:T(8,128)S(1)} %shard_map.68.both) | copy-start | bytes 786436

commit v7 on v5

--- a/solution.py
+++ b/solution.py
@@ -67,8 +67,8 @@
     ext_v, ext_r, grad_v, grad_r,
     p0, p1, a2, a1, vx1, vx2, bx, vy1, vy2, by,
     ex, ey, ez, zd, inv, kk, s1, ss, q2, vz1, vz2, rr, obs, dens, speed, w_plus, w_minus,
-    cs, sl, rl, zs, zr, ys, yr, place, places,
-    fy_s, fy_r, fz_s, fz_r, fl_s, fl_r, rl_s, rl_r, rz_s, rz_r, ry_s, ry_r, at_s, at_r,
+    p_here, obs_here, cs, sl, rl, zs, zr, ys, yr, place, places,
+    fy_s, fy_r, fz_s, fz_r, fl_s, fl_r, rl_s, rl_r, rz_s, rz_r, ry_s, ry_r, at_s, at_r, in_s,
 ):
     block, _, depth = vel_in.shape
     width = p_in.shape[0]
@@ -101,6 +101,15 @@
     pl.when(has_behind)(lambda: greet((a, behind)))
     pl.when(has_line[0])(lambda: greet((a - 1, b)))
     pl.when(has_line[1])(lambda: greet((a + 1, b)))
+    mid = pl.ds(block, block)
+    loads = [
+        pltpu.make_async_copy(rho_in, ext_r.at[mid, mid, :], in_s.at[0]),
+        pltpu.make_async_copy(vel_in, ext_v.at[mid, mid, :], in_s.at[1]),
+        pltpu.make_async_copy(p_in, p_here, in_s.at[2]),
+        pltpu.make_async_copy(obs_in, obs_here, in_s.at[3]),
+    ]
+    for load in loads:
+        load.start()
     one = jnp.int32(1)
     none = jnp.int32(0)
     count = one
@@ -166,8 +175,6 @@
         fwd_y(k, h).start()
         start_line(k, h, 0)
 
-    for k in range(2):
-        exts[k][block:2 * block, block:2 * block, :] = ins[k][...]
     for field in (p0, p1, a2, a1, vx1, vx2, bx):
         field[0:4, :, :] = jnp.zeros((4, width, depth), jnp.float32)
         field[width + 4:width + 8, :, :] = jnp.zeros((4, width, depth), jnp.float32)
@@ -176,10 +183,12 @@
 
     def reorder(i, carry):
         for t in range(turns):
-            p0[i + 4, 8 * t:8 * t + 8, :] = p_in[i, pl.ds(t, 8, turns), :]
-            obs[i, 8 * t:8 * t + 8, :] = obs_in[i, pl.ds(t, 8, turns), :]
+            p0[i + 4, 8 * t:8 * t + 8, :] = p_here[i, pl.ds(t, 8, turns), :]
+            obs[i, 8 * t:8 * t + 8, :] = obs_here[i, pl.ds(t, 8, turns), :]
         return carry
 
+    for load in loads:
+        load.wait()
     lax.fori_loop(0, width, reorder, 0)
     w_plus[...] = band(depth, True)
     w_minus[...] = band(depth, False)
@@ -510,11 +519,11 @@
     both = pl.pallas_call(
         functools.partial(kernel, n_line, n_shot),
         out_shape=jax.ShapeDtypeStruct((2,) + velocity.shape, jnp.float32),
-        in_specs=[pl.BlockSpec(memory_space=pltpu.SMEM)] + [vmem] * 4,
+        in_specs=[pl.BlockSpec(memory_space=pltpu.SMEM)] + [pl.BlockSpec(memory_space=pl.ANY)] * 4,
         out_specs=vmem,
         scratch_shapes=[extended] * 2 + [wide] * 2 + [along_x] * 7 + [plain] * 18
-        + [matrix] * 2 + [scratch(2, 2, block, block, depth)] + [pieces] * 2 + [pair] * 4 + [place, places]
-        + [sem((2, PARTS))] * 4 + [sem((2, PARTS, 2, 2))] * 4 + [sem((2, PARTS))] * 4 + [sem((2,))] * 2,
+        + [matrix] * 2 + [plain] * 2 + [scratch(2, 2, block, block, depth)] + [pieces] * 2 + [pair] * 4 + [place, places]
+        + [sem((2, PARTS))] * 4 + [sem((2, PARTS, 2, 2))] * 4 + [sem((2, PARTS))] * 4 + [sem((2,))] * 2 + [sem((4,))],
         compiler_params=pltpu.CompilerParams(
             collective_id=0, has_side_effects=True, vmem_limit_bytes=56 * 1024 * 1024
         ),

time: 39.5 us -> 39.1 us (0.990)
  Pallas kernels: 38.7 us -> 38.3 us
    pallas_call x1, Pallas kernels: 37.1 us -> 36.6 us  [body(): pl.pallas_call(functools.partial(kernel, n_line, n_shot), out_shape=jax.S...]
where the time goes in v7:
time: 39.1 us; the launch traced here: 38.9 us
  Pallas kernels  38.3 us (98%)
  between operations  0.64 us (2%)
    pallas_call x1, Pallas kernels, body(): pl.pallas_call(functools.partial(kernel, n_line, n_shot), out_shape=jax.S...  36.6 us
    pallas_call x1, Pallas kernels, body(): pl.pallas_call(apart, out_shape=(cells, cells), in_specs=[vmem], out_spec...  1.66 us

profile of v7, /device:TPU:9, one launch (start us, length us, event | category | flops | bytes accessed | tf_op | source)
XLA Modules:
  0.0 38.9 jit_solution(5004364329106674666)
XLA Ops:
  0.6 36.6 %shard_map.68.both = f32[2,16,16,128]{3,2,1,0:T(8,128)} custom-call(s32[2]{0:T(128)} %bitcast.1, f32[16,16,128]{2,1,0:T(8,128)} %vel_in.1, f32[16,16,128]{2,1,0:T(8,128)} %rho_in.1, f32[32,32,128]{2,1,0:T(8,128)} %p_in.1, f32[32,32,128]{2,1,0:T(8,128)} %obs_in.1), custom_call_target="tpu_custom_call" | custom-call | tf_op jit(solution)/shard_map/pallas_call | solution.py:519
  37.3 1.7 %shard_map.69 = (f32[16,16,128]{2,1,0:T(8,128)}, f32[16,16,128]{2,1,0:T(8,128)}) custom-call(f32[2,16,16,128]{3,2,1,0:T(8,128)} %shard_map.68.both), custom_call_target="tpu_custom_call" | custom-call | tf_op jit(solution)/shard_map/pallas_call | solution.py:531

commit v8 on v7

--- a/solution.py
+++ b/solution.py
@@ -13,7 +13,7 @@
 coeffs = (1225.0 / 1024.0, -245.0 / 3072.0, 49.0 / 5120.0, -5.0 / 7168.0)
 time_ratio = 0.1
 wavelet = (20.0, -12.0)
-PARTS = 2
+PARTS = 4
 RB = 4
 RB_Z = 16
 

time: 39.1 us -> 38.8 us (level); the launches traced: 38.9 us -> 38.2 us
  Pallas kernels: 38.3 us -> 37.6 us
    pallas_call x1, Pallas kernels: 36.6 us -> 35.9 us  [body(): pl.pallas_call(functools.partial(kernel, n_line, n_shot), out_shape=jax.S...]
where the time goes in v8:
time: 38.8 us; the launch traced here: 38.2 us
  Pallas kernels  37.6 us (97%)
  between operations  0.64 us (2%)
    pallas_call x1, Pallas kernels, body(): pl.pallas_call(functools.partial(kernel, n_line, n_shot), out_shape=jax.S...  35.9 us
    pallas_call x1, Pallas kernels, body(): pl.pallas_call(apart, out_shape=(cells, cells), in_specs=[vmem], out_spec...  1.66 us

profile of v8, /device:TPU:9, one launch (start us, length us, event | category | flops | bytes accessed | tf_op | source)
XLA Modules:
  0.0 38.2 jit_solution(7922024498396071301)
XLA Ops:
  0.6 35.9 %shard_map.68.both = f32[2,16,16,128]{3,2,1,0:T(8,128)} custom-call(s32[2]{0:T(128)} %bitcast.1, f32[16,16,128]{2,1,0:T(8,128)} %vel_in.1, f32[16,16,128]{2,1,0:T(8,128)} %rho_in.1, f32[32,32,128]{2,1,0:T(8,128)} %p_in.1, f32[32,32,128]{2,1,0:T(8,128)} %obs_in.1), custom_call_target="tpu_custom_call" | custom-call | tf_op jit(solution)/shard_map/pallas_call | solution.py:519
  36.6 1.7 %shard_map.69 = (f32[16,16,128]{2,1,0:T(8,128)}, f32[16,16,128]{2,1,0:T(8,128)}) custom-call(f32[2,16,16,128]{3,2,1,0:T(8,128)} %shard_map.68.both), custom_call_target="tpu_custom_call" | custom-call | tf_op jit(solution)/shard_map/pallas_call | solution.py:531
